TPU v7x, 128 devices: a whole 4x4x4 slice. The times are simulated.
128 devices in a mesh: wide: 8 (over z, core), group: 16 (over x, y).
Axes of the slice: x: 4, y: 4, z: 4, core: 2. Of those that a mesh axis runs over, the one named last changes fastest.
Arguments:
- residual: float32 [262144, 64], P(('wide', 'group')), may hold values from -6 to 6
- panels: float32 [256, 4, 1024], P(('wide', 'group')), may hold values from -1 to 1, as said below
- near_list: int32 [256, 16], P(('wide', 'group')), may hold values from 0 to 255, as said below
- near_len: int32 [256], P(('wide', 'group')), may hold values from 1 to 16
- far_list: int32 [256, 32], P(('wide', 'group')), may hold values from 0 to 255
- basis_far: float32 [256, 32, 1024], P(('wide', 'group')), may hold values from -0.1875 to 0.1875
- coupling: float32 [256, 32, 1024], P(('wide', 'group')), may hold values from -0.375 to 0.375
Outputs:
- basis_one: float32 [262144, 64], P(('wide', 'group'))
- basis_two: float32 [262144, 64], P(('wide', 'group'))
- factors: float32 [6, 64, 64], replicated
Inputs may be any that keep to these rules, and one draw needn't show every extreme that they name: `near_list`: block i lies in group (i // 2) % 16. Entry 0 of row i is i; every other entry is a block of the same group as i. `panels`: coordinates in rows 0 to 2, weights in row 3 are positive.
All inputs are finite; a program needn't handle non-finite values.
Results may differ from a plain program's by a relative error of at most 0.0063.
Values may be sent and summed in bfloat16 or wider, within the bound.
A program may use at most 192 MiB of HBM per device.

v0:
```python
import jax
import jax.numpy as jnp
from jax import lax
from jax.sharding import PartitionSpec as P

HIGH = lax.Precision.HIGHEST


def near_kernel(own, other, weight_mask):
    dist_sq = jnp.zeros((own.shape[1], other.shape[1]), jnp.float32)
    for axis_c in range(3):
        gap = own[axis_c][:, None] - other[axis_c][None, :]
        dist_sq = dist_sq + gap * gap
    return ((other[3] * weight_mask)[None, :] * lax.rsqrt(dist_sq + 0.01)).astype(jnp.bfloat16)


def project(left, right):
    return jnp.dot(left.T, right, precision=HIGH, preferred_element_type=jnp.float32)


def orthonormal(block, lower):
    return lax.linalg.triangular_solve(lower, block, left_side=False, lower=True, transpose_a=True)


def on_device(residual, panels, near_list, near_len, far_list, basis_far, coupling):
    groups = lax.axis_size("group")
    blocks_dev = panels.shape[0]
    width = panels.shape[2]
    rhs = residual.shape[1]
    slot_count = near_list.shape[1]
    total = float(lax.axis_size("wide") * groups * blocks_dev * width)
    group_panels = lax.all_gather(panels, "wide", axis=0, tiled=True)
    local_ids = near_list // blocks_dev // groups * blocks_dev + near_list % blocks_dev
    others = group_panels[local_ids].reshape(blocks_dev * slot_count, 4, width)
    owners = jnp.repeat(panels, slot_count, axis=0)
    masks = (jnp.arange(slot_count)[None, :] < near_len[:, None]).astype(jnp.float32).reshape(-1)
    near_blocks = lax.map(
        lambda item: near_kernel(item[0], item[1], item[2]), (owners, others, masks)
    )
    near_blocks = near_blocks.reshape(blocks_dev, slot_count, width, width)

    def apply(field):
        blocks = field.reshape(blocks_dev, width, rhs)
        rounded = blocks.astype(jnp.bfloat16)
        coeffs = jnp.einsum("bkq,bqr->bkr", basis_far, blocks, precision=HIGH)
        every = lax.all_gather(coeffs, ("wide", "group"), axis=0, tiled=True)
        group_vectors = lax.all_gather(rounded, "wide", axis=0, tiled=True)
        near_vectors = group_vectors[local_ids]
        near = jnp.einsum(
            "bnpq,bnqr->bpr", near_blocks, near_vectors, preferred_element_type=jnp.float32
        )
        stacked = every[far_list].reshape(blocks_dev, -1, rhs)
        inside = jnp.einsum("bkm,bmr->bkr", coupling, stacked, precision=HIGH)
        far = jnp.einsum("bkp,bkr->bpr", basis_far, inside, precision=HIGH)
        return (0.5 * blocks + near + far).reshape(blocks_dev * width, rhs)

    def extend(left, image):
        heads = lax.psum(project(left, image), ("wide", "group")) / total
        fresh = image - jnp.dot(left, heads, precision=HIGH)
        gram = lax.psum(project(fresh, fresh), ("wide", "group")) / total
        lower = jnp.linalg.cholesky(gram)
        return (orthonormal(fresh, lower), heads, lower)

    gram0 = lax.psum(project(residual, residual), ("wide", "group")) / total
    chol0 = jnp.linalg.cholesky(gram0)
    basis0 = orthonormal(residual, chol0)
    basis_one, h01, chol1 = extend(basis0, apply(basis0))
    left = jnp.concatenate([basis0, basis_one], axis=1)
    basis_two, heads, chol2 = extend(left, apply(basis_one))
    factors = jnp.stack([chol0, h01, chol1, heads[:rhs], heads[rhs:], chol2])
    return (basis_one, basis_two, factors)


def solution(mesh):
    return jax.shard_map(
        on_device,
        mesh=mesh,
        in_specs=(
            P(("wide", "group"), None),
            P(("wide", "group"), None, None),
            P(("wide", "group"), None),
            P(("wide", "group")),
            P(("wide", "group"), None),
            P(("wide", "group"), None, None),
            P(("wide", "group"), None, None),
        ),
        out_specs=(P(("wide", "group"), None), P(("wide", "group"), None), P()),
        check_vma=False,
    )
```

profile of v0, /device:TPU:1, one launch (start us, length us, event | category | flops | bytes accessed | tf_op | source)
XLA Modules:
  0.0 670.7 jit_solution(13904823387095397632)
XLA Ops:
  7.3 1.0 copy-done
  8.8 68.9 %psum.35 = f32[64,64]{1,0:T(8,128)S(1)} all-reduce(f32[64,64]{1,0:T(8,128)S(1)} %fusion.37), channel_id=1, replica_groups=mesh['wide'=8,'group'=16] {'wide','group'}, use_global_device_ids=true, to_apply=%region_0.1 | all-reduce | flops 4096 | bytes 32768 | tf_op jit(solution)/shard_map/psum | solution.py:64
  77.8 5.9 cholesky.59
  85.0 4.9 custom-call.7
  90.6 0.7 copy.77
  91.4 2.1 convolution_bitcast_fusion.6
  93.6 13.9 %all_gather.15 = f32[16,4,1024]{2,1,0:T(4,128)S(1)} all-gather(f32[2,4,1024]{2,1,0:T(4,128)S(1)} %copy-done.4), channel_id=1, replica_groups=mesh['wide'=8,'group'=16] {'wide'}, dimensions={0}, use_global_device_ids=true | all-gather | bytes 294912 | tf_op jit(solution)/shard_map/all_gather | solution.py:32
  107.8 0.9 gather_fusion
  108.8 131.3 %while.10 = (s32[]{:T(128)}, bf16[32,1024,1024]{2,1,0:T(8,128)(2,1)}, f32[32,4,1024]{2,1,0:T(4,128)S(1)}, f32[32]{0:T(128)S(1)}, f32[32,4,1024]{2,1,0:T(4,128)S(...) while((s32[]{:T(128)}, bf16[32,1024,1024]{2,1,0:T(8,128)(2,1)}, f32[32,4,1024]{2,1,0:T(4,128)S(1)}, ...), condition=%wide.region_4.7_spmd, body=%wide.region_3.6_spmd.sunk | while | flops 11535365 | bytes 2183349 | solution.py:37
  110.1 2.8 fusion.68
  114.3 2.8 fusion.68
  118.4 2.8 fusion.68
  122.5 2.8 fusion.68
  126.6 2.8 fusion.68
  130.7 2.8 fusion.68
  134.8 2.8 fusion.68
  138.8 2.8 fusion.68
  143.0 2.8 fusion.68
  147.1 2.8 fusion.68
  151.2 2.8 fusion.68
  155.3 2.8 fusion.68
  159.4 2.8 fusion.68
  163.5 2.8 fusion.68
  167.6 2.8 fusion.68
  171.7 2.8 fusion.68
  175.8 2.8 fusion.68
  179.9 2.8 fusion.68
  184.0 2.7 fusion.68
  188.1 2.8 fusion.68
  192.2 2.8 fusion.68
  196.3 2.8 fusion.68
  200.4 2.8 fusion.68
  204.5 2.8 fusion.68
  208.6 2.8 fusion.68
  212.7 2.8 fusion.68
  216.8 2.7 fusion.68
  220.9 2.8 fusion.68
  225.0 2.8 fusion.68
  229.1 2.8 fusion.68
  233.2 2.8 fusion.68
  237.3 2.8 fusion.68
  240.2 4.3 gather_fusion.1
  244.5 30.1 %fusion.6 = f32[2,1024,64]{1,2,0:T(8,128)S(1)} fusion(bf16[2,16,1024,1024]{3,2,1,0:T(8,128)(2,1)} %bitcast.13, bf16[2,16,1024,64]{2,3,1,0:T(8,128)(2,1)} %bitcast.157, f32[8,2,8,1024]{3,2,1,0:T(8,128)S(1)} %bitcast.160), kind=kOutput, calls=%fused_computation.26 | convolution fusion | flops 4295229440 | bytes 72351744 | tf_op jit(solution)/shard_map/bnpq,bnqr->bpr/dot_general | solution.py:49
  274.7 2.8 gather_fusion.2
  279.5 62.3 %psum.36 = f32[64,64]{1,0:T(8,128)S(1)} all-reduce(f32[64,64]{1,0:T(8,128)S(1)} %fusion.34), channel_id=1, replica_groups=mesh['wide'=8,'group'=16] {'wide','group'}, use_global_device_ids=true, to_apply=%region_5.8 | all-reduce | flops 4096 | bytes 32768 | tf_op jit(solution)/shard_map/psum | solution.py:58
  343.0 64.1 %psum.37 = f32[64,64]{1,0:T(8,128)S(1)} all-reduce(f32[64,64]{1,0:T(8,128)S(1)} %fusion.39), channel_id=1, replica_groups=mesh['wide'=8,'group'=16] {'wide','group'}, use_global_device_ids=true, to_apply=%region_6.9 | all-reduce | flops 4096 | bytes 32768 | tf_op jit(solution)/shard_map/psum | solution.py:60
  407.2 5.9 cholesky.70
  414.4 4.9 custom-call.8
  419.9 0.8 copy.76
  421.5 1.2 convolution_bitcast_fusion.5
  423.3 19.8 %all-gather.9.cloned.1.call-done = bf16[16,1024,64]{1,2,0:T(8,128)(2,1)} async-done(((bf16[2,1024,64]{1,2,0:T(8,128)(2,1)}), bf16[16,1024,64]{1,2,0:T(8,128)(2,1)}) %all-gather.9.cloned.1.call-update) | async-done | bytes 2097168 | tf_op jit(solution)/shard_map/all_gather | solution.py:47
  443.1 4.3 gather_fusion.3
  447.5 30.1 %fusion.5 = f32[2,1024,64]{1,2,0:T(8,128)S(1)} fusion(bf16[2,16,1024,1024]{3,2,1,0:T(8,128)(2,1)} %bitcast.13, bf16[2,16,1024,64]{2,3,1,0:T(8,128)(2,1)} %bitcast.156, f32[8,2,8,1024]{3,2,1,0:T(8,128)S(1)} %bitcast.165), kind=kOutput, calls=%fused_computation.24 | convolution fusion | flops 4295229440 | bytes 72351744 | tf_op jit(solution)/shard_map/bnpq,bnqr->bpr/dot_general | solution.py:49
  477.6 35.8 %all-gather.11.cloned.1.call-done = f32[256,32,64]{2,1,0:T(8,128)} async-done(((f32[2,32,64]{2,1,0:T(8,128)}), f32[256,32,64]{2,1,0:T(8,128)}) %all-gather.11.cloned.1.call-update) | async-done | bytes 2097168 | tf_op jit(solution)/shard_map/all_gather | solution.py:46
  513.4 2.8 gather_fusion.4
  516.2 1.6 fusion.40
  518.5 1.0 fusion.7
  519.5 62.8 %psum.38 = f32[128,64]{1,0:T(8,128)S(1)} all-reduce(f32[128,64]{1,0:T(8,128)S(1)} %fusion.7), channel_id=1, replica_groups=mesh['wide'=8,'group'=16] {'wide','group'}, use_global_device_ids=true, to_apply=%region_7.10 | all-reduce | flops 8192 | bytes 65536 | tf_op jit(solution)/shard_map/psum | solution.py:58
  582.4 0.7 convolution_subtract_fusion
  583.7 64.1 %psum.39 = f32[64,64]{1,0:T(8,128)S(1)} all-reduce(f32[64,64]{1,0:T(8,128)S(1)} %fusion.41), channel_id=1, replica_groups=mesh['wide'=8,'group'=16] {'wide','group'}, use_global_device_ids=true, to_apply=%region_8.11 | all-reduce | flops 4096 | bytes 32768 | tf_op jit(solution)/shard_map/psum | solution.py:60
  647.9 5.9 cholesky.81
  655.3 4.9 custom-call.9
  660.2 1.4 convolution_bitcast_fusion
  662.8 1.3 bitcast_dynamic-update-slice_fusion
  (140 shorter events, 56.1 us)
Async XLA Ops:
  7.2 1.0 copy-start
  7.2 86.4 %copy-start.4 = (f32[2,4,1024]{2,1,0:T(4,128)S(1)}, f32[2,4,1024]{2,1,0:T(4,128)}, u32[]{:S(2)}) copy-start(f32[2,4,1024]{2,1,0:T(4,128)} %param.13) | copy-start | bytes 98308
  7.2 100.3 %copy-start.6 = (s32[2,16]{1,0:T(2,128)S(1)}, s32[2,16]{1,0:T(2,128)}, u32[]{:S(2)}) copy-start(s32[2,16]{1,0:T(2,128)} %param.14) | copy-start | bytes 388
  7.2 100.5 %copy-start.8 = (s32[2]{0:T(128)S(1)}, s32[2]{0:T(128)}, u32[]{:S(2)}) copy-start(s32[2]{0:T(128)} %param.15) | copy-start | bytes 28
  7.2 233.0 %all-gather.5.cloned.1.call-start = ((), (), s32[]{:S(2)}) async-start(), calls=%async_computation | async-start | bytes 2359296 | tf_op jit(solution)/shard_map/all_gather | solution.py:47
  91.3 183.4 %all-gather.7.cloned.1.call-start = ((), (), s32[]{:S(2)}) async-start(), calls=%async_computation.1 | async-start | bytes 4227072 | tf_op jit(solution)/shard_map/all_gather | solution.py:46
  93.6 349.6 %all-gather.9.cloned.1.call-start = ((), (), s32[]{:S(2)}) async-start(), calls=%async_computation.2 | async-start | bytes 2359296 | tf_op jit(solution)/shard_map/all_gather | solution.py:47
  108.8 131.3 %copy-start.7 = (s32[2,32]{1,0:T(2,128)S(1)}, s32[2,32]{1,0:T(2,128)}, u32[]{:S(2)}) copy-start(s32[2,32]{1,0:T(2,128)} %param.16) | copy-start | bytes 772
  244.5 33.0 %copy-start.3 = (f32[2,32,1024]{2,1,0:T(8,128)S(1)}, f32[2,32,1024]{2,1,0:T(8,128)}, u32[]{:S(2)}) copy-start(f32[2,32,1024]{2,1,0:T(8,128)} %param.18) | copy-start | bytes 786436
  244.5 33.7 %copy-start.2 = (f32[2,32,1024]{2,1,0:T(8,128)S(1)}, f32[2,32,1024]{2,1,0:T(8,128)}, u32[]{:S(2)}) copy-start(f32[2,32,1024]{2,1,0:T(8,128)} %param.17) | copy-start | bytes 786436
  419.9 162.4 %copy-start.1 = (f32[64,2048]{1,0:T(8,128)}, f32[64,2048]{1,0:T(8,128)S(1)}, u32[]{:S(2)}) copy-start(f32[64,2048]{1,0:T(8,128)S(1)} %fusion.16) | copy-start | bytes 1572868
  420.8 92.6 %all-gather.11.cloned.1.call-start = ((), (), s32[]{:S(2)}) async-start(), calls=%async_computation.3 | async-start | bytes 4227072 | tf_op jit(solution)/shard_map/all_gather | solution.py:46
  423.3 54.2 %copy-start.5 = (f32[6,64,64]{2,1,0:T(8,128)}, f32[6,64,64]{2,1,0:T(8,128)S(1)}, u32[]{:S(2)}) copy-start(f32[6,64,64]{2,1,0:T(8,128)S(1)} %bitcast_dynamic-update-slice_fusion.1) | copy-start | bytes 294916
Sparse Core Ops, SparseCore 0:
  91.5 22.4 all-gather.4
  117.7 66.9 all-gather.6
  420.9 22.1 all-gather.8
  446.1 67.2 all-gather.10
where the time goes:
time: 672 us; the launch traced here: 671 us
  blocking collectives  336 us (50%)
  other arithmetic  149 us (22%)
  matrix products  74.4 us (11%)
  waiting for transfers between devices  55.7 us (8%)
  local copies, waits for them, and re-layouts  40.5 us (6%)
  between operations  14.1 us (2%)
    psum x2, blocking collectives, extend(): gram = lax.psum(project(fresh, fresh), ('wide', 'group')) / total  128 us
    psum x2, blocking collectives, extend(): heads = lax.psum(project(left, image), ('wide', 'group')) / total  125 us
    dynamic_update_slice x32, other arithmetic, on_device(): lax.map(lambda item: near_kernel(item[0], item[1], item[2]), (owners, oth...  89 us
    psum x1, blocking collectives, on_device(): gram0 = lax.psum(project(residual, residual), ('wide', 'group')) / total  68.9 us
    dot_general x2, matrix products, apply(): jnp.einsum('bnpq,bnqr->bpr', near_blocks, near_vectors, preferred_element...  60.2 us
    all_gather x2, waiting for transfers between devices, apply(): every = lax.all_gather(coeffs, ('wide', 'group'), axis=0, tiled=True)  35.9 us
    mul x32, other arithmetic, near_kernel(): other[3] * weight_mask  21.3 us
    dynamic_slice x32, local copies, waits for them, and re-layouts, on_device(): lax.map(lambda item: near_kernel(item[0], item[1], item[2]), (owners, oth...  20.7 us
  transfers between devices with their start and end apart: 4, of which 2 were waited for; matrix products, arithmetic and copies ran while one was open for 31% of the time, Pallas kernels for 0%

commit v1 on v0

--- a/solution.py
+++ b/solution.py
@@ -41,33 +41,50 @@
 
     def apply(field):
         blocks = field.reshape(blocks_dev, width, rhs)
-        rounded = blocks.astype(jnp.bfloat16)
-        coeffs = jnp.einsum("bkq,bqr->bkr", basis_far, blocks, precision=HIGH)
+        high = blocks.astype(jnp.bfloat16)
+        low = (blocks - high.astype(jnp.float32)).astype(jnp.bfloat16)
+        parts = jnp.concatenate([high, low], axis=2)
+        coeffs = jnp.einsum("bkq,bqr->bkr", basis_far, blocks, precision=HIGH).astype(jnp.bfloat16)
         every = lax.all_gather(coeffs, ("wide", "group"), axis=0, tiled=True)
-        group_vectors = lax.all_gather(rounded, "wide", axis=0, tiled=True)
+        group_vectors = lax.all_gather(parts, "wide", axis=0, tiled=True)
         near_vectors = group_vectors[local_ids]
         near = jnp.einsum(
             "bnpq,bnqr->bpr", near_blocks, near_vectors, preferred_element_type=jnp.float32
         )
-        stacked = every[far_list].reshape(blocks_dev, -1, rhs)
+        near = near[:, :, :rhs] + near[:, :, rhs:]
+        stacked = every[far_list].reshape(blocks_dev, -1, rhs).astype(jnp.float32)
         inside = jnp.einsum("bkm,bmr->bkr", coupling, stacked, precision=HIGH)
         far = jnp.einsum("bkp,bkr->bpr", basis_far, inside, precision=HIGH)
-        return (0.5 * blocks + near + far).reshape(blocks_dev * width, rhs)
+        return (near + far).reshape(blocks_dev * width, rhs)
 
-    def extend(left, image):
-        heads = lax.psum(project(left, image), ("wide", "group")) / total
-        fresh = image - jnp.dot(left, heads, precision=HIGH)
-        gram = lax.psum(project(fresh, fresh), ("wide", "group")) / total
-        lower = jnp.linalg.cholesky(gram)
-        return (orthonormal(fresh, lower), heads, lower)
+    def lower_inverse(lower):
+        return lax.linalg.triangular_solve(lower, jnp.eye(rhs, dtype=jnp.float32), left_side=True, lower=True)
 
-    gram0 = lax.psum(project(residual, residual), ("wide", "group")) / total
-    chol0 = jnp.linalg.cholesky(gram0)
-    basis0 = orthonormal(residual, chol0)
-    basis_one, h01, chol1 = extend(basis0, apply(basis0))
-    left = jnp.concatenate([basis0, basis_one], axis=1)
-    basis_two, heads, chol2 = extend(left, apply(basis_one))
-    factors = jnp.stack([chol0, h01, chol1, heads[:rhs], heads[rhs:], chol2])
+    def dot(left, right):
+        return jnp.dot(left, right, precision=HIGH)
+
+    eye = jnp.eye(rhs, dtype=jnp.float32)
+    image = apply(residual)
+    pair = jnp.concatenate([residual, image], axis=1)
+    gram = lax.psum(project(pair, pair), ("wide", "group")) / total
+    image2 = apply(image)
+    chol0 = jnp.linalg.cholesky(gram[:rhs, :rhs])
+    inv0 = lower_inverse(chol0)
+    h01 = dot(dot(inv0, gram[:rhs, rhs:]), inv0.T)
+    chol1 = jnp.linalg.cholesky(dot(dot(inv0, gram[rhs:, rhs:]), inv0.T) - dot(h01.T, h01))
+    inv1 = lower_inverse(chol1)
+    basis0 = dot(residual, inv0.T)
+    mix_new = dot(inv0.T, inv1.T)
+    mix_old = dot(inv0.T, dot(h01, inv1.T))
+    basis_one = dot(image, mix_new) - dot(residual, mix_old)
+    second = dot(image2, mix_new) - dot(image, mix_old)
+    left = jnp.concatenate([basis0, basis_one, second], axis=1)
+    gram = lax.psum(project(left, second), ("wide", "group")) / total
+    heads = gram[: 2 * rhs]
+    chol2 = jnp.linalg.cholesky(gram[2 * rhs :] - dot(heads.T, heads))
+    inv2 = lower_inverse(chol2)
+    basis_two = dot(second - dot(left[:, : 2 * rhs], heads), inv2.T)
+    factors = jnp.stack([chol0, h01 + 0.5 * eye, chol1, heads[:rhs], heads[rhs:] + 0.5 * eye, chol2])
     return (basis_one, basis_two, factors)
 
 

time: 672 us -> 575 us (0.86)
  blocking collectives: 336 us -> 80.3 us
  waiting for transfers between devices: 55.7 us -> 200 us
  matrix products: 74.4 us -> 81.6 us
    psum x5 -> x1, blocking collectives: 322 us -> 65 us  [on_device(): gram = lax.psum(project(left, second), ('wide', 'group')) / total]
    psum x0 -> x1, waiting for transfers between devices: none -> 135 us  [on_device(): gram = lax.psum(project(pair, pair), ('wide', 'group')) / total]
    all_gather x2, waiting for transfers between devices: 19.8 us -> 29.5 us  [apply(): group_vectors = lax.all_gather(parts, 'wide', axis=0, tiled=True)]
  transfers between devices with their start and end apart: 4 -> 5, of which waited for: 2 -> 3; matrix products, arithmetic and copies ran while one was open for 31% -> 30% of each run, Pallas kernels for 0% -> 0%
where the time goes in v1:
time: 575 us; the launch traced here: 574 us
  waiting for transfers between devices  200 us (35%)
  other arithmetic  153 us (27%)
  matrix products  81.6 us (14%)
  blocking collectives  80.3 us (14%)
  local copies, waits for them, and re-layouts  43.8 us (8%)
  between operations  14.3 us (2%)
    psum x1, waiting for transfers between devices, on_device(): gram = lax.psum(project(pair, pair), ('wide', 'group')) / total  135 us
    dynamic_update_slice x32, other arithmetic, on_device(): lax.map(lambda item: near_kernel(item[0], item[1], item[2]), (owners, oth...  89 us
    dot_general x2, matrix products, apply(): jnp.einsum('bnpq,bnqr->bpr', near_blocks, near_vectors, preferred_element...  65.6 us
    psum x1, blocking collectives, on_device(): gram = lax.psum(project(left, second), ('wide', 'group')) / total  65 us
    all_gather x2, waiting for transfers between devices, apply(): every = lax.all_gather(coeffs, ('wide', 'group'), axis=0, tiled=True)  35.6 us
    all_gather x2, waiting for transfers between devices, apply(): group_vectors = lax.all_gather(parts, 'wide', axis=0, tiled=True)  29.5 us
    mul x32, other arithmetic, near_kernel(): other[3] * weight_mask  22.5 us
    dynamic_slice x32, local copies, waits for them, and re-layouts, on_device(): lax.map(lambda item: near_kernel(item[0], item[1], item[2]), (owners, oth...  20.7 us
  transfers between devices with their start and end apart: 5, of which 3 were waited for; matrix products, arithmetic and copies ran while one was open for 30% of the time, Pallas kernels for 0%

profile of v1, /device:TPU:1, one launch (start us, length us, event | category | flops | bytes accessed | tf_op | source)
XLA Modules:
  0.0 573.9 jit_solution(8509944591296657628)
XLA Ops:
  7.3 1.4 copy.33
  8.7 1.3 convolution_convert_fusion.1
  10.2 1.1 pad_maximum_fusion
  11.4 15.4 %all_gather.15 = f32[16,4,1024]{2,1,0:T(4,128)S(1)} all-gather(f32[2,4,1024]{2,1,0:T(4,128)S(1)} %copy-done.4), channel_id=1, replica_groups=mesh['wide'=8,'group'=16] {'wide'}, dimensions={0}, use_global_device_ids=true | all-gather | bytes 294912 | tf_op jit(solution)/shard_map/all_gather | solution.py:32
  27.0 0.9 gather_fusion
  28.0 132.5 %while.10 = (s32[]{:T(128)}, bf16[32,1024,1024]{2,1,0:T(8,128)(2,1)}, f32[32,4,1024]{2,1,0:T(4,128)S(1)}, f32[32]{0:T(128)S(1)}, f32[32,4,1024]{2,1,0:T(4,128)S(...) while((s32[]{:T(128)}, bf16[32,1024,1024]{2,1,0:T(8,128)(2,1)}, f32[32,4,1024]{2,1,0:T(4,128)S(1)}, ...), condition=%wide.region_1.2_spmd, body=%wide.region_0.1_spmd.sunk | while | flops 11535365 | bytes 2183349 | solution.py:37
  29.4 2.8 fusion.98
  33.6 2.8 fusion.98
  37.7 2.8 fusion.98
  41.9 2.8 fusion.98
  46.0 2.8 fusion.98
  50.1 2.8 fusion.98
  54.3 2.8 fusion.98
  58.4 2.8 fusion.98
  62.5 2.8 fusion.98
  66.7 2.8 fusion.98
  70.8 2.8 fusion.98
  75.0 2.8 fusion.98
  79.1 2.8 fusion.98
  83.2 2.8 fusion.98
  87.4 2.8 fusion.98
  90.8 0.7 dynamic-slice_multiply_fusion.2
  91.5 2.8 fusion.98
  95.6 2.8 fusion.98
  99.8 2.8 fusion.98
  104.0 2.7 fusion.98
  108.1 2.8 fusion.98
  112.2 2.8 fusion.98
  116.4 2.7 fusion.98
  120.5 2.8 fusion.98
  124.6 2.8 fusion.98
  128.8 2.8 fusion.98
  132.9 2.8 fusion.98
  137.1 2.7 fusion.98
  141.2 2.8 fusion.98
  145.3 2.8 fusion.98
  149.5 2.7 fusion.98
  153.6 2.8 fusion.98
  157.8 2.8 fusion.98
  160.6 2.2 gather_fusion.2
  163.2 7.2 %gather_fusion.1 = bf16[32,1024,128]{2,1,0:T(8,128)(2,1)} fusion(bf16[16,1024,128]{2,1,0:T(8,128)(2,1)} %all-gather.5.cloned.1.call-done, s32[1024]{0:T(1024)S(1)} %pad_clamp_fusion.1), kind=kCustom, calls=%fused_computation.1 | custom fusion | bytes 16777344 | tf_op jit(solution)/shard_map/gather | solution.py:50
  170.4 32.8 %convolution_bitcast_fusion.3 = f32[2,1024,128]{1,2,0:T(8,128)S(1)} fusion(bf16[2,16,1024,1024]{3,2,1,0:T(8,128)(2,1)} %bitcast.9, bf16[2,16,1024,128]{3,2,1,0:T(8,128)(2,1)} %bitcast.147), kind=kOutput, calls=%fused_computation.26 | convolution fusion | flops 8589934592 | bytes 76546048 | tf_op jit(solution)/shard_map/bnpq,bnqr->bpr/dot_general | solution.py:51
  203.3 1.4 subtract_convert_fusion.1
  204.7 1.6 fusion.11
  206.4 1.2 fusion.10
  207.8 1.0 pad_maximum_fusion.1
  208.8 1.0 copy.43
  209.8 135.2 %all-reduce.2.cloned.1.call-done = f32[128,128]{0,1:T(8,128)} async-done(((f32[128,128]{0,1:T(8,128)}), f32[128,128]{0,1:T(8,128)}) %all-reduce.2.cloned.1.call-update) | async-done | bytes 65552 | tf_op jit(solution)/shard_map/psum | solution.py:69
  345.0 0.8 broadcast_multiply_fusion.1
  346.0 5.8 %cholesky.59 = f32[64,64]{1,0:T(8,128)S(1)} custom-call(f32[64,64]{1,0:T(8,128)S(1)} %fusion.40), custom_call_target="Cholesky" | custom-call | tf_op jit(solution)/shard_map/jit(cholesky)/cholesky | solution.py:71
  353.1 4.9 custom-call.7
  360.1 5.9 %cholesky.70 = f32[64,64]{1,0:T(8,128)S(1)} custom-call(f32[64,64]{1,0:T(8,128)S(1)} %fusion.38), custom_call_target="Cholesky" | custom-call | tf_op jit(solution)/shard_map/jit(cholesky)/cholesky | solution.py:74
  367.3 4.9 custom-call.8
  375.7 35.5 %all-gather.11.cloned.1.call-done = bf16[256,32,64]{2,1,0:T(8,128)(2,1)} async-done(((bf16[2,32,64]{2,1,0:T(8,128)(2,1)}), bf16[256,32,64]{2,1,0:T(8,128)(2,1)}) %all-gather.11.cloned.1.call-update) | async-done | bytes 1048592 | tf_op jit(solution)/shard_map/all_gather | solution.py:48
  411.2 2.2 gather_fusion.4
  413.8 29.4 %all-gather.9.cloned.1.call-done = bf16[16,1024,128]{2,1,0:T(8,128)(2,1)} async-done(((bf16[2,1024,128]{2,1,0:T(8,128)(2,1)}), bf16[16,1024,128]{2,1,0:T(8,128)(2,1)}) %all-gather.9.cloned.1.call-update) | async-done | bytes 4194320 | tf_op jit(solution)/shard_map/all_gather | solution.py:49
  443.3 7.4 %gather_fusion.3 = bf16[32,1024,128]{2,1,0:T(8,128)(2,1)} fusion(bf16[16,1024,128]{2,1,0:T(8,128)(2,1)} %all-gather.9.cloned.1.call-done, s32[1024]{0:T(1024)S(1)} %pad_clamp_fusion.1), kind=kCustom, calls=%fused_computation.3 | custom fusion | bytes 16777344 | tf_op jit(solution)/shard_map/gather | solution.py:50
  450.7 32.8 %convolution_bitcast_fusion.2 = f32[2,1024,128]{1,2,0:T(8,128)S(1)} fusion(bf16[2,16,1024,1024]{3,2,1,0:T(8,128)(2,1)} %bitcast.9, bf16[2,16,1024,128]{3,2,1,0:T(8,128)(2,1)} %bitcast.146), kind=kOutput, calls=%fused_computation.25 | convolution fusion | flops 8589934592 | bytes 76546048 | tf_op jit(solution)/shard_map/bnpq,bnqr->bpr/dot_general | solution.py:51
  485.4 1.4 fusion.1
  486.8 65.0 %psum.15 = f32[192,64]{1,0:T(8,128)S(1)} all-reduce(f32[192,64]{1,0:T(8,128)S(1)} %fusion.1), channel_id=1, replica_groups=mesh['wide'=8,'group'=16] {'wide','group'}, use_global_device_ids=true, to_apply=%region_5.8 | all-reduce | flops 12288 | bytes 98304 | tf_op jit(solution)/shard_map/psum | solution.py:82
  551.7 0.7 convolution_subtract_fusion
  552.9 5.9 %cholesky.81 = f32[64,64]{1,0:T(8,128)S(1)} custom-call(f32[64,64]{1,0:T(8,128)S(1)} %copy.49), custom_call_target="Cholesky" | custom-call | tf_op jit(solution)/shard_map/jit(cholesky)/cholesky | solution.py:84
  560.1 4.9 custom-call.9
  566.0 1.4 fusion.53
  (149 shorter events, 57.1 us)
Async XLA Ops:
  7.2 1.5 copy-start
  7.2 4.2 copy-start.4
  7.2 19.6 %copy-start.6 = (s32[2,16]{1,0:T(2,128)S(1)}, s32[2,16]{1,0:T(2,128)}, u32[]{:S(2)}) copy-start(s32[2,16]{1,0:T(2,128)} %param.14) | copy-start | bytes 388
  7.2 19.7 %copy-start.8 = (s32[2]{0:T(128)S(1)}, s32[2]{0:T(128)}, u32[]{:S(2)}) copy-start(s32[2]{0:T(128)} %param.15) | copy-start | bytes 28
  7.2 153.4 %all-gather.7.cloned.1.call-start = ((), (), s32[]{:S(2)}) async-start(), calls=%async_computation.1 | async-start | bytes 2113536 | tf_op jit(solution)/shard_map/all_gather | solution.py:48
  10.0 153.2 %all-gather.5.cloned.1.call-start = ((), (), s32[]{:S(2)}) async-start(), calls=%async_computation | async-start | bytes 4718592 | tf_op jit(solution)/shard_map/all_gather | solution.py:49
  11.3 333.7 %all-reduce.2.cloned.1.call-start = ((), (), s32[]{:S(2)}) async-start(), calls=%async_computation.2 | async-start | bytes 131072 | tf_op jit(solution)/shard_map/psum | solution.py:69
  28.0 132.5 %copy-start.7 = (s32[2,32]{1,0:T(2,128)S(1)}, s32[2,32]{1,0:T(2,128)}, u32[]{:S(2)}) copy-start(s32[2,32]{1,0:T(2,128)} %param.16) | copy-start | bytes 772
  28.0 134.8 %copy-start.3 = (f32[2,32,1024]{2,1,0:T(8,128)S(1)}, f32[2,32,1024]{2,1,0:T(8,128)}, u32[]{:S(2)}) copy-start(f32[2,32,1024]{2,1,0:T(8,128)} %param.18) | copy-start | bytes 786436
  170.4 34.3 %copy-start.1 = (f32[2048,64]{0,1:T(8,128)S(1)}, f32[2048,64]{0,1:T(8,128)}, u32[]{:S(2)}) copy-start(f32[2048,64]{0,1:T(8,128)} %param.12) | copy-start | bytes 1572868
  206.3 204.9 %all-gather.11.cloned.1.call-start = ((), (), s32[]{:S(2)}) async-start(), calls=%async_computation.4 | async-start | bytes 2113536 | tf_op jit(solution)/shard_map/all_gather | solution.py:48
  207.6 235.7 %all-gather.9.cloned.1.call-start = ((), (), s32[]{:S(2)}) async-start(), calls=%async_computation.3 | async-start | bytes 4718592 | tf_op jit(solution)/shard_map/all_gather | solution.py:49
  375.7 176.1 %copy-start.2 = (f32[2048,64]{0,1:T(8,128)}, f32[2048,64]{0,1:T(8,128)S(1)}, u32[]{:S(2)}) copy-start(f32[2048,64]{0,1:T(8,128)S(1)} %convolution_subtract_fusion.2) | copy-start | bytes 1572868
  566.0 1.4 copy-start.5
Sparse Core Ops, SparseCore 0:
  11.6 68.8 all-gather.6
  82.8 29.7 all-gather.4
  206.5 138.5 all-reduce.1
  348.3 62.8 all-gather.10
  413.5 29.7 all-gather.8

commit v2 on v0

v2 whole, which is shorter than its diff:
```python
import jax
import jax.numpy as jnp
from jax import lax
from jax.experimental import pallas as pl
from jax.experimental.pallas import tpu as pltpu
from jax.sharding import PartitionSpec as P

HIGH = lax.Precision.HIGHEST
MESH = pl.DeviceIdType.MESH
F32 = jnp.float32
BF16 = jnp.bfloat16

B = 1024
R = 64
K = 32
NF = 32
DEPTH = 32
CHUNKS = 16
RESIDENT = 3
KEPT = 2 * RESIDENT
SMALL = 2.0 ** -30

NN_DIMS = (((1,), (0,)), ((), ()))
NT_DIMS = (((1,), (1,)), ((), ()))
TN_DIMS = (((0,), (0,)), ((), ()))


def exact(left, right, dims=NN_DIMS):
    return lax.dot_general(left, right, dims, precision=HIGH, preferred_element_type=F32)


def fast(left, right, dims=NN_DIMS):
    return lax.dot_general(left, right, dims, preferred_element_type=F32)


def two_parts(value):
    high = value.astype(BF16)
    return high, (value - high.astype(F32)).astype(BF16)


def three_parts(value):
    first = value.astype(BF16).astype(F32)
    rest = value - first
    second = rest.astype(BF16).astype(F32)
    return first, second, rest - second


class Place:
    def __init__(self):
        wide = lax.axis_index("wide")
        group = lax.axis_index("group")
        self.z, self.core = wide // 2, wide % 2
        self.x, self.y = group // 4, group % 4

    def wide(self, dz, flip):
        return (self.z + dz + 4) % 4 * 2 + (self.core + flip) % 2

    def device(self, dz=0, flip=0, dx=0, dy=0):
        return (self.wide(dz, flip), (self.x + dx + 4) % 4 * 4 + (self.y + dy + 4) % 4)


def remote(source, target, send, recv, device):
    return pltpu.make_async_remote_copy(
        src_ref=source, dst_ref=target, send_sem=send, recv_sem=recv, device_id=device, device_id_type=MESH
    )


class GroupGather:
    MOVES = (
        (0, 0, 2, 0, 1),
        (0, 0, 1, 1, 0),
        (0, 1, 1, 1, 0),
        (0, 1, 1, -1, 0),
        (0, 0, 1, -1, 0),
        (-1, 0, 1, 1, 0),
        (1, 1, 1, -1, 0),
        (-1, 0, 2, 0, 1),
        (1, 0, 2, 0, 1),
        (2, 0, 1, 0, 1),
        (2, 1, 1, 0, 1),
    )

    def __init__(self, place, buf, send, recv):
        self.place, self.buf, self.send, self.recv = place, buf, send, recv

    def copy(self, n):
        dz, first, count, to_z, flip = self.MOVES[n]
        part = self.buf.at[self.place.wide(dz, 0), pl.ds(first, count)]
        return remote(part, part, self.send.at[n], self.recv.at[n], self.place.device(to_z, flip))

    def start(self, *moves):
        for n in moves:
            self.copy(n).start()

    def wait(self, *moves):
        for n in moves:
            dz, first, count, to_z, flip = self.MOVES[n]
            part = self.buf.at[self.place.wide(dz - to_z, flip), pl.ds(first, count)]
            remote(part, part, self.send.at[n], self.recv.at[n], self.place.device(to_z, flip)).wait_recv()

    def finish(self):
        for n in range(len(self.MOVES)):
            self.copy(n).wait_send()


class CoefficientGather:
    def __init__(self, place, buf, send, recv):
        self.place, self.buf, self.send, self.recv = place, buf, send, recv

    def span(self, stage, back):
        here = self.place
        core, x, y, z = here.core, here.x, here.y, here.z
        if stage == 0:
            return ((core * 4 + x) * 4 + y) * 4 + (z - back + 4) % 4, 1
        if stage == 1:
            return ((core * 4 + x) * 4 + (y - back + 4) % 4) * 4, 4
        if stage == 2:
            return (core * 4 + (x - back + 4) % 4) * 16, 16
        return (core + back) % 2 * 64, 64

    def copy(self, stage, step, back):
        first, count = self.span(stage, back)
        part = self.buf.at[pl.ds(first, count)]
        target = (dict(dz=step), dict(dy=step), dict(dx=step), dict(flip=step))[stage]
        n = stage * 3 + step - 1
        return remote(part, part, self.send.at[n], self.recv.at[n], self.place.device(**target))

    def steps(self, stage):
        return (1,) if stage == 3 else (1, 2, 3)

    def start(self, stage):
        for step in self.steps(stage):
            self.copy(stage, step, 0).start()

    def wait(self, stage):
        for step in self.steps(stage):
            self.copy(stage, step, step).wait_recv()

    def finish(self):
        for stage in range(4):
            for step in self.steps(stage):
                self.copy(stage, step, 0).wait_send()


class AllReduce:
    def __init__(self, place, part, other, rings, full, send, recv):
        self.place, self.part, self.other, self.rings, self.full = place, part, other, rings, full
        self.send, self.recv = send, recv

    def swap(self):
        here = self.place
        return remote(
            self.part.at[1 - here.core], self.other, self.send.at[0], self.recv.at[0], here.device(flip=1)
        )

    def spot(self, stage):
        return (self.place.z, self.place.y, self.place.x)[stage]

    def copy(self, stage, step, back):
        slot = self.rings.at[stage, (self.spot(stage) - back + 4) % 4]
        target = (dict(dz=step), dict(dy=step), dict(dx=step))[stage]
        n = 1 + stage * 3 + step - 1
        return remote(slot, slot, self.send.at[n], self.recv.at[n], self.place.device(**target))

    def share(self, back):
        half = self.full.at[(self.place.core + back) % 2]
        return remote(half, half, self.send.at[10], self.recv.at[10], self.place.device(flip=1))

    def start(self):
        self.swap().start()

    def ring(self, stage):
        if stage == 0:
            self.swap().wait_recv()
            total = self.part[self.place.core] + self.other[...]
        else:
            for step in (1, 2, 3):
                self.copy(stage - 1, step, step).wait_recv()
            rings = self.rings
            total = (rings[stage - 1, 0] + rings[stage - 1, 1]) + (rings[stage - 1, 2] + rings[stage - 1, 3])
        if stage < 3:
            self.rings[stage, self.spot(stage)] = total
            for step in (1, 2, 3):
                self.copy(stage, step, 0).start()
        else:
            self.full[self.place.core] = total
            self.share(0).start()

    def wait(self):
        self.share(1).wait_recv()

    def finish(self):
        self.swap().wait_send()
        for stage in range(3):
            for step in (1, 2, 3):
                self.copy(stage, step, 0).wait_send()
        self.share(0).wait_send()


def cholesky(gram):
    lane = lax.broadcasted_iota(jnp.int32, (R, 2 * R), 1)
    row = lax.broadcasted_iota(jnp.int32, (R, 2 * R), 0)
    start = jnp.where(lane < R, jnp.where(lane == row, 1.0, 0.0), pltpu.roll(gram, R, 1))
    blocks = [start[8 * t : 8 * t + 8] for t in range(8)]
    rows = []
    for k in range(R):
        t, o = divmod(k, 8)
        line = blocks[t][o : o + 1]
        pivot = line[:, R + k : R + k + 1]
        root = lax.rsqrt(pivot)
        root = root * (1.5 - 0.5 * pivot * root * root)
        line = line * root
        rows.append(line)
        for u in range(t, 8):
            blocks[u] = blocks[u] - (blocks[u][:, R + k : R + k + 1] * root) * line
    done = jnp.concatenate(rows, axis=0)
    inverse = done[:, :R]
    upper = jnp.where(lane >= row, pltpu.roll(done, R, 1), 0.0)[:, :R]
    return inverse, upper


def step_kernel(
    res_ref, panels_ref, near_ref, len_ref, far_ref, basis_ref, coupling_ref,
    one_ref, two_ref, factors_ref, stored_ref,
    field, space, vectors, vectors2, coeffs, coeffs2, blocks, acc, counts, rows, own, coupled, stacked,
    part, other, rings, full, part2, other2, rings2, full2, left,
    near_send, near_recv, far_send, far_recv, sum_send, sum_recv, keep_sem, load_sem,
):
    here = Place()
    me = here.wide(0, 0)
    total = float(128 * 2 * B)

    barrier = pltpu.get_barrier_semaphore()
    partners = [here.device(flip=1)]
    for step in (1, 2, 3):
        partners += [here.device(dz=step), here.device(dy=step), here.device(dx=step)]
    for partner in partners:
        pl.semaphore_signal(barrier, inc=1, device_id=partner, device_id_type=MESH)

    for b in range(2):
        point = [panels_ref[b, a : a + 1, :] for a in range(3)]
        weight = jnp.maximum(panels_ref[b, 3:4, :], SMALL)
        scale = 1.0 / (weight * weight)
        square = point[0] * point[0] + point[1] * point[1] + point[2] * point[2]
        pairs = [(three_parts(-2.0 * point[a] * scale), three_parts(point[a])) for a in range(3)]
        pairs.append((three_parts(scale), three_parts(square)))
        line = 0
        for theirs, mine in pairs:
            for m, n in ((0, 0), (0, 1), (1, 0), (0, 2), (1, 1), (2, 0)):
                rows[0, line : line + 1, :] = theirs[m]
                rows[1, line : line + 1, :] = mine[n]
                line += 1
        for value in three_parts((square + 0.01) * scale):
            rows[0, line : line + 1, :] = value
            rows[1, line : line + 1, :] = jnp.ones((1, B), F32)
            line += 1
        rows[0, line:DEPTH, :] = jnp.zeros((DEPTH - line, B), F32)
        rows[1, line:DEPTH, :] = jnp.zeros((DEPTH - line, B), F32)
        space[me, b] = rows[0].astype(BF16)
        own[b] = rows[1].astype(BF16)

    def spread(source, target):
        for b in range(2):
            value = source[:, b * B : (b + 1) * B]
            weight = panels_ref[b, 3:4, :]
            high, low = two_parts(value * (weight / jnp.maximum(weight, SMALL)))
            target[me, b, :R] = high
            target[me, b, R:] = low

    def project(source, target):
        zero = jnp.zeros((R, B), F32)
        first = jnp.concatenate([source[:, :B], zero], axis=0)
        second = jnp.concatenate([zero, source[:, B:]], axis=0)
        value = exact(basis_ref[0], first, NT_DIMS) + exact(basis_ref[1], second, NT_DIMS)
        target[((here.core * 4 + here.x) * 4 + here.y) * 4 + here.z] = value.astype(BF16)

    near_space = GroupGather(here, space, near_send.at[0], near_recv.at[0])
    near_first = GroupGather(here, vectors, near_send.at[1], near_recv.at[1])
    near_second = GroupGather(here, vectors2, near_send.at[2], near_recv.at[2])
    far_first = CoefficientGather(here, coeffs, far_send.at[0], far_recv.at[0])
    far_second = CoefficientGather(here, coeffs2, far_send.at[1], far_recv.at[1])
    sum_first = AllReduce(here, part, other, rings, full, sum_send.at[0], sum_recv.at[0])
    sum_second = AllReduce(here, part2, other2, rings2, full2, sum_send.at[1], sum_recv.at[1])

    field[0:R, :] = res_ref[...]
    spread(field[0:R, :], vectors)
    pl.semaphore_wait(barrier, len(partners))
    near_space.start(0, 1, 3, 2, 4)
    near_first.start(0, 1, 3, 2, 4)
    project(field[0:R, :], coeffs)
    far_first.start(0)

    for i in range(2):
        ids = near_ref[i : i + 1, :]
        ids = (ids >> 5) * 2 + (ids & 1)
        wanted = lax.broadcasted_iota(jnp.int32, (16, 16), 0)
        slot = lax.broadcasted_iota(jnp.int32, (16, 16), 1)
        hit = jnp.where((ids == wanted) & (slot < len_ref[i]), 1.0, 0.0)
        counts[i] = jnp.broadcast_to(jnp.sum(hit, axis=1, keepdims=True), (16, 128))
        high, low = two_parts(coupling_ref[i])
        coupled[i, :K] = high
        coupled[i, K:] = low
        acc[i] = jnp.zeros((2 * R, B), F32)

    def source_of(c):
        s = c // 2

        def since(k):
            return (s + 8 - k) // 8

        flip = since(1) - since(2) + since(4) - since(6) + since(7)
        dz = since(2) + 2 * (since(3) - since(4)) + 2 * (since(5) - since(6)) + since(6)
        return here.wide(dz, flip)

    def slot_of(c):
        late = (c + CHUNKS - KEPT) // CHUNKS
        return c + late * (KEPT + c % 2 - c)

    def keep(c):
        return pltpu.make_async_copy(blocks.at[slot_of(c)], stored_ref.at[c - KEPT], keep_sem.at[c % 2])

    def load(c):
        return pltpu.make_async_copy(stored_ref.at[c - KEPT], blocks.at[slot_of(c)], load_sem.at[c % 2])

    def run(first, last, generate, values, events):
        def chunk(c, carry):
            for at, event in events.items():
                pl.when(c == at)(event)
            w, slot, i = source_of(c), slot_of(c), c % 2
            if generate:
                @pl.when(c >= KEPT + 2)
                def _():
                    keep(c - 2).wait()
            elif values is vectors2:
                @pl.when(c >= KEPT)
                def _():
                    load(c).wait()
            result = acc[i] if values is not None else None
            for b in range(2):
                if generate:
                    near = lax.rsqrt(fast(space[w, b], own[i], TN_DIMS)).astype(BF16)
                    blocks[slot, b] = near
                else:
                    near = blocks[slot, b]
                if values is not None:
                    times = counts[i, pl.ds(w * 2 + b, 1), :][:, :1]
                    result = result + times * fast(values[w, b], near)
            if values is not None:
                acc[i] = result
            if generate:
                @pl.when(c >= KEPT)
                def _():
                    keep(c).start()
            elif values is vectors2:
                @pl.when((c >= KEPT) & (c < CHUNKS - 2))
                def _():
                    load(c + 2).start()
            return carry

        lax.fori_loop(first, last, chunk, 0)

    def far_part(gathered, i):
        lane = lax.broadcasted_iota(jnp.int32, (K, 2 * R), 1)

        def entry(n, carry):
            block = far_ref[i, n]
            device, half = block >> 1, block & 1
            wide, group = device >> 4, device & 15
            slot = ((wide & 1) * 16 + group) * 4 + (wide >> 1)
            value = gathered[slot].astype(F32)
            stacked[pl.ds(pl.multiple_of(n * K, K), K), :] = jnp.where(lane // R == half, value, 0.0).astype(BF16)
            return carry

        lax.fori_loop(0, NF, entry, 0)
        inside = fast(coupled[i], stacked[...])
        inside = inside[:K] + inside[K:]
        result = exact(inside, basis_ref[i], TN_DIMS)
        return result[:R] + result[R:]

    def finish_rows(gathered, first):
        for i in range(2):
            near = acc[i]
            field[first : first + R, i * B : (i + 1) * B] = near[:R] + near[R:] + far_part(gathered, i)
            acc[i] = jnp.zeros((2 * R, B), F32)

    def before_2():
        near_space.wait(0)
        near_first.wait(0)
        near_space.wait(1, 3)
        near_space.start(5, 6)
        far_first.wait(0)
        far_first.start(1)

    run(0, 4, True, vectors, {2: before_2})

    def before_4():
        near_space.wait(2, 4)
        near_space.start(7, 8)

    def before_6():
        near_first.wait(1, 3)
        near_first.start(5, 6)
        far_first.wait(1)
        far_first.start(2)

    run(4, 8, True, None, {4: before_4, 6: before_6})
    near_first.wait(2, 4)
    near_first.start(7, 8)
    run(4, 8, False, vectors, {})

    def before_8():
        near_space.wait(5, 6)
        near_space.start(9, 10)
        near_space.wait(7, 8)
        near_first.wait(7, 8)

    def before_12():
        near_first.wait(5, 6)
        near_first.start(9, 10)
        near_space.wait(9, 10)
        far_first.wait(2)
        far_first.start(3)

    def before_14():
        near_first.wait(9, 10)

    run(8, 16, True, vectors, {8: before_8, 12: before_12, 14: before_14})
    far_first.wait(3)
    keep(CHUNKS - 2).wait()
    keep(CHUNKS - 1).wait()
    finish_rows(coeffs, R)

    spread(field[R : 2 * R, :], vectors2)
    near_second.start(0, 1, 3, 2, 4)
    load(KEPT).start()
    load(KEPT + 1).start()
    project(field[R : 2 * R, :], coeffs2)
    far_second.start(0)
    pair = field[0 : 2 * R, :]
    gram = exact(pair, pair, NT_DIMS) * (1.0 / total)
    part[0] = gram[:R]
    part[1] = gram[R:]
    sum_first.start()

    def second_2():
        sum_first.ring(0)
        far_second.wait(0)
        far_second.start(1)
        near_second.wait(0)

    run(0, 4, False, vectors2, {2: second_2})
    sum_first.ring(1)
    near_second.wait(1, 3)
    near_second.start(5, 6)
    sum_first.ring(2)
    far_second.wait(1)
    far_second.start(2)
    sum_first.ring(3)
    sum_first.wait()
    inverse0, upper0 = cholesky(full[0])
    cross = full[1][:, :R]
    square = pltpu.roll(full[1], R, 1)[:, :R]
    cross = exact(exact(inverse0, cross), inverse0, NT_DIMS)
    square = exact(exact(inverse0, square), inverse0, NT_DIMS) - exact(cross, cross, NT_DIMS)
    inverse1, upper1 = cholesky(jnp.concatenate([square, jnp.zeros((R, R), F32)], axis=1))
    mix_new = exact(inverse1, inverse0)
    mix_old = exact(exact(inverse1, cross), inverse0)
    eye = jnp.where(
        lax.broadcasted_iota(jnp.int32, (R, R), 0) == lax.broadcasted_iota(jnp.int32, (R, R), 1), 0.5, 0.0
    )
    factors_ref[0] = upper0
    factors_ref[1] = cross + eye
    factors_ref[2] = upper1
    left[0:R, :] = exact(inverse0, field[0:R, :])
    left[R : 2 * R, :] = exact(mix_new, field[R : 2 * R, :]) - exact(mix_old, field[0:R, :])
    one_ref[...] = left[R : 2 * R, :]

    def second_4():
        near_second.wait(2, 4)
        near_second.start(7, 8)

    def second_8():
        near_second.wait(5, 6)
        near_second.start(9, 10)
        near_second.wait(7, 8)
        far_second.wait(2)
        far_second.start(3)

    def second_14():
        near_second.wait(9, 10)

    run(4, 16, False, vectors2, {4: second_4, 8: second_8, 14: second_14})
    far_second.wait(3)
    finish_rows(coeffs2, 2 * R)

    left[2 * R :, :] = exact(mix_new, field[2 * R :, :]) - exact(mix_old, field[R : 2 * R, :])
    newest = left[2 * R :, :]
    part2[0] = exact(newest, left[0 : 2 * R, :], NT_DIMS) * (1.0 / total)
    part2[1] = jnp.concatenate([exact(newest, newest, NT_DIMS) * (1.0 / total), jnp.zeros((R, R), F32)], axis=1)
    sum_second.start()
    for stage in range(4):
        sum_second.ring(stage)
    sum_second.wait()
    heads = full2[0]
    rest = full2[1][:, :R] - exact(heads, heads, NT_DIMS)
    inverse2, upper2 = cholesky(jnp.concatenate([rest, jnp.zeros((R, R), F32)], axis=1))
    factors_ref[3] = heads[:, :R]
    factors_ref[4] = pltpu.roll(heads, R, 1)[:, :R] + eye
    factors_ref[5] = upper2
    two_ref[...] = exact(inverse2, newest - exact(heads, left[0 : 2 * R, :]))

    for gather in (near_space, near_first, near_second, far_first, far_second, sum_first, sum_second):
        gather.finish()


def on_device(residual, panels, near_list, near_len, far_list, basis_far, coupling):
    vmem = pl.BlockSpec(memory_space=pltpu.VMEM)
    smem = pl.BlockSpec(memory_space=pltpu.SMEM)
    wide = jax.ShapeDtypeStruct((R, 2 * B), F32)
    sums = [
        pltpu.VMEM((2, R, 2 * R), F32),
        pltpu.VMEM((R, 2 * R), F32),
        pltpu.VMEM((3, 4, R, 2 * R), F32),
        pltpu.VMEM((2, R, 2 * R), F32),
    ]
    one, two, factors, _ = pl.pallas_call(
        step_kernel,
        out_shape=(
            wide,
            wide,
            jax.ShapeDtypeStruct((6, R, R), F32),
            jax.ShapeDtypeStruct((CHUNKS - KEPT, 2, B, B), BF16),
        ),
        in_specs=[vmem, vmem, vmem, smem, smem, vmem, vmem],
        out_specs=(vmem, vmem, vmem, pl.BlockSpec(memory_space=pl.ANY)),
        scratch_shapes=[
            pltpu.VMEM((3 * R, 2 * B), F32),
            pltpu.VMEM((8, 2, DEPTH, B), BF16),
            pltpu.VMEM((8, 2, 2 * R, B), BF16),
            pltpu.VMEM((8, 2, 2 * R, B), BF16),
            pltpu.VMEM((128, K, 2 * R), BF16),
            pltpu.VMEM((128, K, 2 * R), BF16),
            pltpu.VMEM((KEPT + 2, 2, B, B), BF16),
            pltpu.VMEM((2, 2 * R, B), F32),
            pltpu.VMEM((2, 16, 128), F32),
            pltpu.VMEM((2, DEPTH, B), F32),
            pltpu.VMEM((2, DEPTH, B), BF16),
            pltpu.VMEM((2, 2 * K, NF * K), BF16),
            pltpu.VMEM((NF * K, 2 * R), BF16),
            *sums,
            *sums,
            pltpu.VMEM((3 * R, 2 * B), F32),
            pltpu.SemaphoreType.DMA((3, 11)),
            pltpu.SemaphoreType.DMA((3, 11)),
            pltpu.SemaphoreType.DMA((2, 10)),
            pltpu.SemaphoreType.DMA((2, 10)),
            pltpu.SemaphoreType.DMA((2, 11)),
            pltpu.SemaphoreType.DMA((2, 11)),
            pltpu.SemaphoreType.DMA((2,)),
            pltpu.SemaphoreType.DMA((2,)),
        ],
        compiler_params=pltpu.CompilerParams(
            collective_id=0, has_side_effects=True, vmem_limit_bytes=62 * 2**20
        ),
        cost_estimate=pl.CostEstimate(flops=17_000_000_000, bytes_accessed=80_000_000, transcendentals=33_554_432),
    )(residual.T, panels, near_list, near_len, far_list, basis_far, coupling)
    return (one.T, two.T, jnp.transpose(factors, (0, 2, 1)))


def solution(mesh):
    return jax.shard_map(
        on_device,
        mesh=mesh,
        in_specs=(
            P(("wide", "group"), None),
            P(("wide", "group"), None, None),
            P(("wide", "group"), None),
            P(("wide", "group")),
            P(("wide", "group"), None),
            P(("wide", "group"), None, None),
            P(("wide", "group"), None, None),
        ),
        out_specs=(P(("wide", "group"), None), P(("wide", "group"), None), P()),
        check_vma=False,
    )
```

time: 672 us -> 149 us (0.22)
  blocking collectives: 336 us -> 0 us
  other arithmetic: 149 us -> 0 us
  Pallas kernels: 0 us -> 142 us
  matrix products: 74.4 us -> 0 us
  waiting for transfers between devices: 55.7 us -> 0 us
  local copies, waits for them, and re-layouts: 40.5 us -> 5.46 us
  between operations: 14.1 us -> 0.64 us
    psum x5 -> x0, blocking collectives: 322 us -> none  [the longest x2 128 us: extend(): gram = lax.psum(project(fresh, fresh), ('wide', 'group')) / total]
    pallas_call x0 -> x1, Pallas kernels: none -> 142 us  [on_device(): pl.pallas_call(step_kernel, out_shape=(wide, wide, jax.ShapeDtypeStruct((...]
    dynamic_update_slice x32 -> x0, other arithmetic: 89 us -> none  [on_device(): lax.map(lambda item: near_kernel(item[0], item[1], item[2]), (owners, oth...]
    dot_general x15 -> x0, matrix products: 71.7 us -> none  [the longest x2 60.2 us: apply(): jnp.einsum('bnpq,bnqr->bpr', near_blocks, near_vectors, preferred_element...]
    all_gather x4 -> x0, waiting for transfers between devices: 55.6 us -> none  [the longest x2 35.9 us: apply(): every = lax.all_gather(coeffs, ('wide', 'group'), axis=0, tiled=True)]
    another operation x16 -> x0, other arithmetic: 37.7 us -> none  [the longest x6 16.7 us: orthonormal(): lax.linalg.triangular_solve(lower, block, left_side=False, lower=True, tr...]
    mul x32 -> x0, other arithmetic: 21.3 us -> none  [near_kernel(): other[3] * weight_mask]
    dynamic_slice x32 -> x0, local copies, waits for them, and re-layouts: 20.7 us -> none  [on_device(): lax.map(lambda item: near_kernel(item[0], item[1], item[2]), (owners, oth...]
  transfers between devices with their start and end apart: 4 -> 0, of which waited for: 2 -> 0; matrix products, arithmetic and copies ran while one was open for 31% -> 0% of each run, Pallas kernels for 0% -> 0%
where the time goes in v2:
time: 149 us; the launch traced here: 148 us
  Pallas kernels  142 us (95%)
  local copies, waits for them, and re-layouts  5.46 us (4%)
    pallas_call x1, Pallas kernels, on_device(): pl.pallas_call(step_kernel, out_shape=(wide, wide, jax.ShapeDtypeStruct((...  142 us
    unnamed x3, local copies, waits for them, and re-layouts  5.46 us

profile of v2, /device:TPU:1, one launch (start us, length us, event | category | flops | bytes accessed | tf_op | source)
XLA Modules:
  0.0 148.2 jit_solution(11951435246548241446)
XLA Ops:
  0.6 142.1 %shard_map.94 = (f32[64,2048]{1,0:T(8,128)}, f32[64,2048]{1,0:T(8,128)}, f32[6,64,64]{2,1,0:T(8,128)}, bf16[10,2,1024,1024]{3,2,1,0:T(8,128)(2,1)}) custom-call(f32[64,2048]{1,0:T(8,128)} %bitcast.7, f32[2,4,1024]{2,1,0:T(4,128)} %panels_ref.1, s32[2,16]{1,0:T(2,128)} %near_ref.1, s32[2]{0:T(128)} %len_ref.1, s32[2,32]{1,0:T(2,128)} %far_ref.1, ...), custom_call_target="tpu_custom_call" | custom-call | flops 16999999488 | bytes 80000000 | tf_op jit(solution)/shard_map/pallas_call | solution.py:526
  142.7 1.7 %copy.10 = f32[6,64,64]{2,1,0:T(8,128)} copy(f32[6,64,64]{1,2,0:T(8,128)} %bitcast.6) | data formatting | bytes 196608
  144.4 1.9 %copy.13 = f32[2048,64]{0,1:T(8,128)} copy(f32[2048,64]{0,1:T(8,128)} %bitcast.5) | data formatting | bytes 1048576
  146.3 1.9 %copy.14 = f32[2048,64]{0,1:T(8,128)} copy(f32[2048,64]{0,1:T(8,128)} %bitcast.4) | data formatting | bytes 1048576

commit v3 on v2

--- a/solution.py
+++ b/solution.py
@@ -16,7 +16,7 @@
 NF = 32
 DEPTH = 32
 CHUNKS = 16
-RESIDENT = 3
+RESIDENT = 4
 KEPT = 2 * RESIDENT
 SMALL = 2.0 ** -30
 
@@ -36,6 +36,13 @@
 def two_parts(value):
     high = value.astype(BF16)
     return high, (value - high.astype(F32)).astype(BF16)
+
+
+def close(left, right, dims=NN_DIMS):
+    left_high, left_low = two_parts(left)
+    right_high, right_low = two_parts(right)
+    cross = fast(left_high, right_low, dims) + fast(left_low, right_high, dims)
+    return fast(left_high, right_high, dims) + cross
 
 
 def three_parts(value):
@@ -67,25 +74,28 @@
 
 class GroupGather:
     MOVES = (
-        (0, 0, 2, 0, 1),
-        (0, 0, 1, 1, 0),
-        (0, 1, 1, 1, 0),
-        (0, 1, 1, -1, 0),
-        (0, 0, 1, -1, 0),
-        (-1, 0, 1, 1, 0),
-        (1, 1, 1, -1, 0),
-        (-1, 0, 2, 0, 1),
-        (1, 0, 2, 0, 1),
-        (2, 0, 1, 0, 1),
-        (2, 1, 1, 0, 1),
+        (0, 0, 0, 1),
+        (0, 1, 0, 1),
+        (0, 0, 1, 0),
+        (0, 1, 1, 0),
+        (0, 1, -1, 0),
+        (0, 0, -1, 0),
+        (-1, 0, 1, 0),
+        (1, 1, -1, 0),
+        (-1, 0, 0, 1),
+        (-1, 1, 0, 1),
+        (1, 0, 0, 1),
+        (1, 1, 0, 1),
+        (2, 0, 0, 1),
+        (2, 1, 0, 1),
     )
 
     def __init__(self, place, buf, send, recv):
         self.place, self.buf, self.send, self.recv = place, buf, send, recv
 
     def copy(self, n):
-        dz, first, count, to_z, flip = self.MOVES[n]
-        part = self.buf.at[self.place.wide(dz, 0), pl.ds(first, count)]
+        dz, block, to_z, flip = self.MOVES[n]
+        part = self.buf.at[self.place.wide(dz, 0), block]
         return remote(part, part, self.send.at[n], self.recv.at[n], self.place.device(to_z, flip))
 
     def start(self, *moves):
@@ -94,8 +104,8 @@
 
     def wait(self, *moves):
         for n in moves:
-            dz, first, count, to_z, flip = self.MOVES[n]
-            part = self.buf.at[self.place.wide(dz - to_z, flip), pl.ds(first, count)]
+            dz, block, to_z, flip = self.MOVES[n]
+            part = self.buf.at[self.place.wide(dz - to_z, flip), block]
             remote(part, part, self.send.at[n], self.recv.at[n], self.place.device(to_z, flip)).wait_recv()
 
     def finish(self):
@@ -203,28 +213,45 @@
     start = jnp.where(lane < R, jnp.where(lane == row, 1.0, 0.0), pltpu.roll(gram, R, 1))
     blocks = [start[8 * t : 8 * t + 8] for t in range(8)]
     rows = []
-    for k in range(R):
-        t, o = divmod(k, 8)
-        line = blocks[t][o : o + 1]
-        pivot = line[:, R + k : R + k + 1]
-        root = lax.rsqrt(pivot)
-        root = root * (1.5 - 0.5 * pivot * root * root)
-        line = line * root
-        rows.append(line)
-        for u in range(t, 8):
-            blocks[u] = blocks[u] - (blocks[u][:, R + k : R + k + 1] * root) * line
+    for t in range(8):
+        cols = [
+            {u: jnp.broadcast_to(blocks[u][:, R + k : R + k + 1], (8, 2 * R)) for u in range(t, 8)}
+            for k in range(8 * t, 8 * t + 8)
+        ]
+        for j in range(8):
+            root = lax.rsqrt(cols[j][t][j : j + 1])
+            line = blocks[t][j : j + 1] * root
+            rows.append(line)
+            scaled = {u: cols[j][u] * root for u in range(t, 8)}
+            for later in range(j + 1, 8):
+                factor = scaled[t][later : later + 1]
+                for u in range(t, 8):
+                    cols[later][u] = cols[later][u] - scaled[u] * factor
+            for u in range(t, 8):
+                blocks[u] = blocks[u] - scaled[u] * line
     done = jnp.concatenate(rows, axis=0)
     inverse = done[:, :R]
     upper = jnp.where(lane >= row, pltpu.roll(done, R, 1), 0.0)[:, :R]
     return inverse, upper
 
 
+def pack(wide, square):
+    low = jnp.concatenate([square[: R // 2], square[R // 2 :]], axis=1)
+    return jnp.concatenate([wide, low], axis=0).reshape(2, 48, 2 * R)
+
+
+def unpack(value):
+    value = value.reshape(96, 2 * R)
+    low = value[R:]
+    return value[:R], jnp.concatenate([low, pltpu.roll(low, R, 1)], axis=0)
+
+
 def step_kernel(
     res_ref, panels_ref, near_ref, len_ref, far_ref, basis_ref, coupling_ref,
-    one_ref, two_ref, factors_ref, stored_ref,
+    left_ref, sums_ref, small_ref, stored_ref,
     field, space, vectors, vectors2, coeffs, coeffs2, blocks, acc, counts, rows, own, coupled, stacked,
     part, other, rings, full, part2, other2, rings2, full2, left,
-    near_send, near_recv, far_send, far_recv, sum_send, sum_recv, keep_sem, load_sem,
+    near_send, near_recv, far_send, far_recv, sum_send, sum_recv, keep_sem, load_sem, left_sem,
 ):
     here = Place()
     me = here.wide(0, 0)
@@ -259,19 +286,15 @@
         space[me, b] = rows[0].astype(BF16)
         own[b] = rows[1].astype(BF16)
 
-    def spread(source, target):
-        for b in range(2):
-            value = source[:, b * B : (b + 1) * B]
-            weight = panels_ref[b, 3:4, :]
-            high, low = two_parts(value * (weight / jnp.maximum(weight, SMALL)))
-            target[me, b, :R] = high
-            target[me, b, R:] = low
+    def spread(source, target, b):
+        weight = panels_ref[b, 3:4, :]
+        target[me, b] = (source[:, b * B : (b + 1) * B] * (weight / jnp.maximum(weight, SMALL))).astype(BF16)
 
     def project(source, target):
         zero = jnp.zeros((R, B), F32)
         first = jnp.concatenate([source[:, :B], zero], axis=0)
         second = jnp.concatenate([zero, source[:, B:]], axis=0)
-        value = exact(basis_ref[0], first, NT_DIMS) + exact(basis_ref[1], second, NT_DIMS)
+        value = close(basis_ref[0], first, NT_DIMS) + close(basis_ref[1], second, NT_DIMS)
         target[((here.core * 4 + here.x) * 4 + here.y) * 4 + here.z] = value.astype(BF16)
 
     near_space = GroupGather(here, space, near_send.at[0], near_recv.at[0])
@@ -283,10 +306,11 @@
     sum_second = AllReduce(here, part2, other2, rings2, full2, sum_send.at[1], sum_recv.at[1])
 
     field[0:R, :] = res_ref[...]
-    spread(field[0:R, :], vectors)
+    spread(res_ref, vectors, 0)
+    spread(res_ref, vectors, 1)
     pl.semaphore_wait(barrier, len(partners))
-    near_space.start(0, 1, 3, 2, 4)
-    near_first.start(0, 1, 3, 2, 4)
+    near_space.start(2, 4, 3, 5, 0, 1)
+    near_first.start(2, 4, 3, 5, 0, 1)
     project(field[0:R, :], coeffs)
     far_first.start(0)
 
@@ -300,10 +324,15 @@
         high, low = two_parts(coupling_ref[i])
         coupled[i, :K] = high
         coupled[i, K:] = low
-        acc[i] = jnp.zeros((2 * R, B), F32)
+        acc[i] = jnp.zeros((R, B), F32)
+
+    def row_of(c):
+        late = c // 8
+        return (1 - late) * (c % 2) + late * (c // 4 - 2)
 
     def source_of(c):
-        s = c // 2
+        late = c // 8
+        s = (1 - late) * (c // 2) + late * (4 + c % 4)
 
         def since(k):
             return (s + 8 - k) // 8
@@ -326,7 +355,7 @@
         def chunk(c, carry):
             for at, event in events.items():
                 pl.when(c == at)(event)
-            w, slot, i = source_of(c), slot_of(c), c % 2
+            w, slot, i = source_of(c), slot_of(c), row_of(c)
             if generate:
                 @pl.when(c >= KEPT + 2)
                 def _():
@@ -371,146 +400,186 @@
             stacked[pl.ds(pl.multiple_of(n * K, K), K), :] = jnp.where(lane // R == half, value, 0.0).astype(BF16)
             return carry
 
-        lax.fori_loop(0, NF, entry, 0)
+        lax.fori_loop(0, NF, entry, 0, unroll=8)
         inside = fast(coupled[i], stacked[...])
         inside = inside[:K] + inside[K:]
-        result = exact(inside, basis_ref[i], TN_DIMS)
+        result = close(inside, basis_ref[i], TN_DIMS)
         return result[:R] + result[R:]
 
-    def finish_rows(gathered, first):
-        for i in range(2):
-            near = acc[i]
-            field[first : first + R, i * B : (i + 1) * B] = near[:R] + near[R:] + far_part(gathered, i)
-            acc[i] = jnp.zeros((2 * R, B), F32)
+    def finish_row(gathered, first, i):
+        field[first : first + R, i * B : (i + 1) * B] = acc[i] + far_part(gathered, i)
+        acc[i] = jnp.zeros((R, B), F32)
 
     def before_2():
-        near_space.wait(0)
-        near_first.wait(0)
-        near_space.wait(1, 3)
-        near_space.start(5, 6)
+        near_space.wait(0, 1)
+        near_first.wait(0, 1)
+
+    def before_3():
+        near_space.wait(2, 4)
+        near_space.start(6, 7)
         far_first.wait(0)
         far_first.start(1)
 
-    run(0, 4, True, vectors, {2: before_2})
+    run(0, 4, True, vectors, {2: before_2, 3: before_3})
 
     def before_4():
-        near_space.wait(2, 4)
-        near_space.start(7, 8)
+        near_space.wait(3, 5)
+        near_space.start(8, 9, 10, 11)
 
     def before_6():
-        near_first.wait(1, 3)
-        near_first.start(5, 6)
+        near_first.wait(2, 4)
+        near_first.start(6, 7)
         far_first.wait(1)
         far_first.start(2)
 
-    run(4, 8, True, None, {4: before_4, 6: before_6})
-    near_first.wait(2, 4)
-    near_first.start(7, 8)
+    def before_7():
+        near_space.wait(6, 7)
+        near_space.start(12, 13)
+
+    run(4, 8, True, None, {4: before_4, 6: before_6, 7: before_7})
+    near_first.wait(3, 5)
+    near_first.start(8, 9, 10, 11)
     run(4, 8, False, vectors, {})
 
     def before_8():
-        near_space.wait(5, 6)
-        near_space.start(9, 10)
-        near_space.wait(7, 8)
-        near_first.wait(7, 8)
-
-    def before_12():
-        near_first.wait(5, 6)
-        near_first.start(9, 10)
-        near_space.wait(9, 10)
+        near_space.wait(8, 9, 10, 11)
+        near_first.wait(8, 9, 10, 11)
+        near_first.wait(6, 7)
+        near_first.start(12, 13)
+
+    def before_10():
+        near_space.wait(12, 13)
         far_first.wait(2)
         far_first.start(3)
 
+    def before_11():
+        near_first.wait(12, 13)
+
+    def before_12():
+        far_first.wait(3)
+        finish_row(coeffs, R, 0)
+        spread(field[R : 2 * R, :], vectors2, 0)
+        near_second.start(2, 5, 0)
+
     def before_14():
-        near_first.wait(9, 10)
-
-    run(8, 16, True, vectors, {8: before_8, 12: before_12, 14: before_14})
-    far_first.wait(3)
+        near_second.wait(2)
+        near_second.start(6)
+
+    def before_15():
+        near_second.wait(5)
+        near_second.start(8, 10)
+
+    run(8, 16, True, vectors, {8: before_8, 10: before_10, 11: before_11, 12: before_12, 14: before_14, 15: before_15})
+    finish_row(coeffs, R, 1)
+
+    spread(field[R : 2 * R, :], vectors2, 1)
+    near_second.start(4, 3, 1)
     keep(CHUNKS - 2).wait()
+    load(KEPT).start()
     keep(CHUNKS - 1).wait()
-    finish_rows(coeffs, R)
-
-    spread(field[R : 2 * R, :], vectors2)
-    near_second.start(0, 1, 3, 2, 4)
-    load(KEPT).start()
     load(KEPT + 1).start()
+    gram = close(field[R : 2 * R, :], field[0 : 2 * R, :], NT_DIMS) * (1.0 / total)
+    first_gram = close(field[0:R, :], field[0:R, :], NT_DIMS) * (1.0 / total)
+    part[...] = pack(gram, first_gram)
+    sum_first.start()
     project(field[R : 2 * R, :], coeffs2)
     far_second.start(0)
-    pair = field[0 : 2 * R, :]
-    gram = exact(pair, pair, NT_DIMS) * (1.0 / total)
-    part[0] = gram[:R]
-    part[1] = gram[R:]
-    sum_first.start()
 
     def second_2():
         sum_first.ring(0)
+        near_second.wait(0, 1)
+
+    def second_4():
         far_second.wait(0)
         far_second.start(1)
-        near_second.wait(0)
-
-    run(0, 4, False, vectors2, {2: second_2})
-    sum_first.ring(1)
-    near_second.wait(1, 3)
-    near_second.start(5, 6)
-    sum_first.ring(2)
-    far_second.wait(1)
-    far_second.start(2)
-    sum_first.ring(3)
+        near_second.wait(4)
+        near_second.start(7)
+        near_second.wait(3)
+        near_second.start(9, 11)
+        near_second.wait(6)
+        near_second.start(12)
+        sum_first.ring(1)
+
+    def second_8():
+        near_second.wait(8, 9, 10, 11)
+        far_second.wait(1)
+        far_second.start(2)
+
+    def second_9():
+        sum_first.ring(2)
+
+    def second_10():
+        near_second.wait(7)
+        near_second.start(13)
+
+    def second_11():
+        near_second.wait(12, 13)
+
+    def second_14():
+        sum_first.ring(3)
+
+    run(
+        0, 16, False, vectors2,
+        {2: second_2, 4: second_4, 8: second_8, 9: second_9, 10: second_10, 11: second_11, 14: second_14},
+    )
+    far_second.wait(2)
+    far_second.start(3)
     sum_first.wait()
-    inverse0, upper0 = cholesky(full[0])
-    cross = full[1][:, :R]
-    square = pltpu.roll(full[1], R, 1)[:, :R]
+    gram, first_gram = unpack(full[...])
+    inverse0, upper0 = cholesky(first_gram)
+    cross = gram[:, :R]
+    square = pltpu.roll(gram, R, 1)[:, :R]
     cross = exact(exact(inverse0, cross), inverse0, NT_DIMS)
     square = exact(exact(inverse0, square), inverse0, NT_DIMS) - exact(cross, cross, NT_DIMS)
     inverse1, upper1 = cholesky(jnp.concatenate([square, jnp.zeros((R, R), F32)], axis=1))
     mix_new = exact(inverse1, inverse0)
     mix_old = exact(exact(inverse1, cross), inverse0)
-    eye = jnp.where(
-        lax.broadcasted_iota(jnp.int32, (R, R), 0) == lax.broadcasted_iota(jnp.int32, (R, R), 1), 0.5, 0.0
-    )
-    factors_ref[0] = upper0
-    factors_ref[1] = cross + eye
-    factors_ref[2] = upper1
-    left[0:R, :] = exact(inverse0, field[0:R, :])
-    left[R : 2 * R, :] = exact(mix_new, field[R : 2 * R, :]) - exact(mix_old, field[0:R, :])
-    one_ref[...] = left[R : 2 * R, :]
-
-    def second_4():
-        near_second.wait(2, 4)
-        near_second.start(7, 8)
-
-    def second_8():
-        near_second.wait(5, 6)
-        near_second.start(9, 10)
-        near_second.wait(7, 8)
-        far_second.wait(2)
-        far_second.start(3)
-
-    def second_14():
-        near_second.wait(9, 10)
-
-    run(4, 16, False, vectors2, {4: second_4, 8: second_8, 14: second_14})
+    small_ref[0] = upper0
+    small_ref[1] = cross
+    small_ref[2] = upper1
+    left[0:R, :] = close(inverse0, field[0:R, :])
+    mix = jnp.concatenate([-mix_old, mix_new], axis=1)
+    left[R : 2 * R, :] = close(mix, field[0 : 2 * R, :])
+    early = pltpu.make_async_copy(left.at[pl.ds(0, 2 * R)], left_ref.at[pl.ds(0, 2 * R)], left_sem.at[0])
+    early.start()
     far_second.wait(3)
-    finish_rows(coeffs2, 2 * R)
-
-    left[2 * R :, :] = exact(mix_new, field[2 * R :, :]) - exact(mix_old, field[R : 2 * R, :])
+    finish_row(coeffs2, 2 * R, 0)
+    finish_row(coeffs2, 2 * R, 1)
+
+    left[2 * R :, :] = close(mix, field[R:, :])
     newest = left[2 * R :, :]
-    part2[0] = exact(newest, left[0 : 2 * R, :], NT_DIMS) * (1.0 / total)
-    part2[1] = jnp.concatenate([exact(newest, newest, NT_DIMS) * (1.0 / total), jnp.zeros((R, R), F32)], axis=1)
+    late = pltpu.make_async_copy(left.at[pl.ds(2 * R, R)], left_ref.at[pl.ds(2 * R, R)], left_sem.at[1])
+    late.start()
+    heads = close(newest, left[0 : 2 * R, :], NT_DIMS) * (1.0 / total)
+    part2[...] = pack(heads, close(newest, newest, NT_DIMS) * (1.0 / total))
     sum_second.start()
     for stage in range(4):
         sum_second.ring(stage)
+    for gather in (near_space, near_first, near_second, far_first, far_second, sum_first):
+        gather.finish()
+    early.wait()
+    late.wait()
     sum_second.wait()
-    heads = full2[0]
-    rest = full2[1][:, :R] - exact(heads, heads, NT_DIMS)
-    inverse2, upper2 = cholesky(jnp.concatenate([rest, jnp.zeros((R, R), F32)], axis=1))
-    factors_ref[3] = heads[:, :R]
-    factors_ref[4] = pltpu.roll(heads, R, 1)[:, :R] + eye
-    factors_ref[5] = upper2
-    two_ref[...] = exact(inverse2, newest - exact(heads, left[0 : 2 * R, :]))
-
-    for gather in (near_space, near_first, near_second, far_first, far_second, sum_first, sum_second):
-        gather.finish()
+    sums_ref[...] = full2[...]
+    sum_second.finish()
+
+
+def last_kernel(left_ref, sums_ref, small_ref, one_ref, two_ref, factors_ref):
+    one_ref[...] = left_ref[R : 2 * R, :]
+    heads, rest = unpack(sums_ref[...])
+    rest = rest[:, :R] - exact(heads, heads, NT_DIMS)
+    inverse, upper = cholesky(jnp.concatenate([rest, jnp.zeros((R, R), F32)], axis=1))
+    mix = jnp.concatenate([-exact(inverse, heads[:, :R]), -exact(inverse, pltpu.roll(heads, R, 1)[:, :R])], axis=1)
+    two_ref[...] = close(mix, left_ref[: 2 * R, :]) + close(inverse, left_ref[2 * R :, :])
+    row = lax.broadcasted_iota(jnp.int32, (R, R), 0)
+    lane = lax.broadcasted_iota(jnp.int32, (R, R), 1)
+    half = jnp.where(row == lane, 0.5, 0.0)
+    factors_ref[0] = small_ref[0].T
+    factors_ref[1] = small_ref[1].T + half
+    factors_ref[2] = small_ref[2].T
+    factors_ref[3] = heads[:, :R].T
+    factors_ref[4] = pltpu.roll(heads, R, 1)[:, :R].T + half
+    factors_ref[5] = upper.T
 
 
 def on_device(residual, panels, near_list, near_len, far_list, basis_far, coupling):
@@ -518,30 +587,30 @@
     smem = pl.BlockSpec(memory_space=pltpu.SMEM)
     wide = jax.ShapeDtypeStruct((R, 2 * B), F32)
     sums = [
-        pltpu.VMEM((2, R, 2 * R), F32),
-        pltpu.VMEM((R, 2 * R), F32),
-        pltpu.VMEM((3, 4, R, 2 * R), F32),
-        pltpu.VMEM((2, R, 2 * R), F32),
+        pltpu.VMEM((2, 48, 2 * R), F32),
+        pltpu.VMEM((48, 2 * R), F32),
+        pltpu.VMEM((3, 4, 48, 2 * R), F32),
+        pltpu.VMEM((2, 48, 2 * R), F32),
     ]
-    one, two, factors, _ = pl.pallas_call(
+    left, sums_all, small, _ = pl.pallas_call(
         step_kernel,
         out_shape=(
-            wide,
-            wide,
-            jax.ShapeDtypeStruct((6, R, R), F32),
+            jax.ShapeDtypeStruct((3 * R, 2 * B), F32),
+            jax.ShapeDtypeStruct((2, 48, 2 * R), F32),
+            jax.ShapeDtypeStruct((3, R, R), F32),
             jax.ShapeDtypeStruct((CHUNKS - KEPT, 2, B, B), BF16),
         ),
         in_specs=[vmem, vmem, vmem, smem, smem, vmem, vmem],
-        out_specs=(vmem, vmem, vmem, pl.BlockSpec(memory_space=pl.ANY)),
+        out_specs=(pl.BlockSpec(memory_space=pl.ANY), vmem, vmem, pl.BlockSpec(memory_space=pl.ANY)),
         scratch_shapes=[
             pltpu.VMEM((3 * R, 2 * B), F32),
             pltpu.VMEM((8, 2, DEPTH, B), BF16),
-            pltpu.VMEM((8, 2, 2 * R, B), BF16),
-            pltpu.VMEM((8, 2, 2 * R, B), BF16),
+            pltpu.VMEM((8, 2, R, B), BF16),
+            pltpu.VMEM((8, 2, R, B), BF16),
             pltpu.VMEM((128, K, 2 * R), BF16),
             pltpu.VMEM((128, K, 2 * R), BF16),
             pltpu.VMEM((KEPT + 2, 2, B, B), BF16),
-            pltpu.VMEM((2, 2 * R, B), F32),
+            pltpu.VMEM((2, R, B), F32),
             pltpu.VMEM((2, 16, 128), F32),
             pltpu.VMEM((2, DEPTH, B), F32),
             pltpu.VMEM((2, DEPTH, B), BF16),
@@ -550,12 +619,13 @@
             *sums,
             *sums,
             pltpu.VMEM((3 * R, 2 * B), F32),
-            pltpu.SemaphoreType.DMA((3, 11)),
-            pltpu.SemaphoreType.DMA((3, 11)),
+            pltpu.SemaphoreType.DMA((3, 14)),
+            pltpu.SemaphoreType.DMA((3, 14)),
             pltpu.SemaphoreType.DMA((2, 10)),
             pltpu.SemaphoreType.DMA((2, 10)),
             pltpu.SemaphoreType.DMA((2, 11)),
             pltpu.SemaphoreType.DMA((2, 11)),
+            pltpu.SemaphoreType.DMA((2,)),
             pltpu.SemaphoreType.DMA((2,)),
             pltpu.SemaphoreType.DMA((2,)),
         ],
@@ -564,7 +634,14 @@
         ),
         cost_estimate=pl.CostEstimate(flops=17_000_000_000, bytes_accessed=80_000_000, transcendentals=33_554_432),
     )(residual.T, panels, near_list, near_len, far_list, basis_far, coupling)
-    return (one.T, two.T, jnp.transpose(factors, (0, 2, 1)))
+    one, two, factors = pl.pallas_call(
+        last_kernel,
+        out_shape=(wide, wide, jax.ShapeDtypeStruct((6, R, R), F32)),
+        in_specs=[vmem, vmem, vmem],
+        out_specs=(vmem, vmem, vmem),
+        cost_estimate=pl.CostEstimate(flops=150_000_000, bytes_accessed=3_000_000, transcendentals=64),
+    )(left, sums_all, small)
+    return (one.T, two.T, factors)
 
 
 def solution(mesh):

time: 149 us -> 104 us (0.70)
  Pallas kernels: 142 us -> 103 us
  local copies, waits for them, and re-layouts: 5.46 us -> 0 us
    pallas_call x1 -> x2, Pallas kernels: 142 us -> 103 us  [the longest x1 98.2 us: on_device(): pl.pallas_call(step_kernel, out_shape=(jax.ShapeDtypeStruct((3 * R, 2 * B...]
    unnamed x3 -> x0, local copies, waits for them, and re-layouts: 5.46 us -> none
where the time goes in v3:
time: 104 us
  Pallas kernels  103 us (99%)
    pallas_call x1, Pallas kernels, on_device(): pl.pallas_call(step_kernel, out_shape=(jax.ShapeDtypeStruct((3 * R, 2 * B...  98.2 us
    pallas_call x1, Pallas kernels, on_device(): pl.pallas_call(last_kernel, out_shape=(wide, wide, jax.ShapeDtypeStruct((...  5.19 us

profile of v3, /device:TPU:1, one launch (start us, length us, event | category | flops | bytes accessed | tf_op | source)
XLA Modules:
  0.0 104.0 jit_solution(2769841360475744344)
XLA Ops:
  0.6 98.2 %shard_map.94 = (f32[192,2048]{1,0:T(8,128)}, f32[2,48,128]{2,1,0:T(8,128)}, f32[3,64,64]{2,1,0:T(8,128)}, bf16[8,2,1024,1024]{3,2,1,0:T(8,128)(2,1)}) custom-call(f32[64,2048]{1,0:T(8,128)} %bitcast.3, f32[2,4,1024]{2,1,0:T(4,128)} %panels_ref.1, s32[2,16]{1,0:T(2,128)} %near_ref.1, s32[2]{0:T(128)} %len_ref.1, s32[2,32]{1,0:T(2,128)} %far_ref.1, ...), custom_call_target="tpu_custom_call" | custom-call | flops 16999999488 | bytes 80000000 | tf_op jit(solution)/shard_map/pallas_call | solution.py:595
  98.8 5.2 %shard_map.95 = (f32[64,2048]{1,0:T(8,128)}, f32[64,2048]{1,0:T(8,128)}, f32[6,64,64]{2,1,0:T(8,128)}) custom-call(f32[192,2048]{1,0:T(8,128)} %get-tuple-element.9.left_ref, f32[2,48,128]{2,1,0:T(8,128)} %get-tuple-element.10.sums_ref, f32[3,64,64]{2,1,0:T(8,128)} %get-tuple-element.11.small_ref), custom_call_target="tpu_custom_call" | custom-call | flops 150000000 | bytes 3000000 | tf_op jit(solution)/shard_map/pallas_call | solution.py:637

commit v4 on v3

--- a/solution.py
+++ b/solution.py
@@ -15,9 +15,7 @@
 K = 32
 NF = 32
 DEPTH = 32
-CHUNKS = 16
-RESIDENT = 4
-KEPT = 2 * RESIDENT
+PAIRS = 8
 SMALL = 2.0 ** -30
 
 NN_DIMS = (((1,), (0,)), ((), ()))
@@ -117,39 +115,63 @@
     def __init__(self, place, buf, send, recv):
         self.place, self.buf, self.send, self.recv = place, buf, send, recv
 
-    def span(self, stage, back):
-        here = self.place
-        core, x, y, z = here.core, here.x, here.y, here.z
+    def axes(self, half):
+        return (self.place.y, self.place.x) if half else (self.place.x, self.place.y)
+
+    def slot(self, half):
+        a, b = self.axes(half)
+        return ((self.place.core * 4 + a) * 4 + b) * 4 + self.place.z
+
+    def move(self, half, stage, step, back, flip=0):
+        a, b = self.axes(half)
+        core, z = (self.place.core + flip) % 2, self.place.z
         if stage == 0:
-            return ((core * 4 + x) * 4 + y) * 4 + (z - back + 4) % 4, 1
-        if stage == 1:
-            return ((core * 4 + x) * 4 + (y - back + 4) % 4) * 4, 4
+            first, count = ((core * 4 + a) * 4 + b) * 4 + (z - back + 4) % 4, 1
+            target = dict(dz=step)
+        elif stage == 1:
+            first, count = ((core * 4 + a) * 4 + (b - back + 4) % 4) * 4, 4
+            target = dict(dx=step) if half else dict(dy=step)
+        elif stage == 2:
+            first, count = (core * 4 + (a - back + 4) % 4) * 16, 16
+            target = dict(dy=step) if half else dict(dx=step)
+        else:
+            first, count = (core * 4 + (a - step + 4) % 4) * 16, 16
+            target = dict(flip=1)
+        n = half * 13 + stage * 3 + (step if stage == 3 else step - 1)
+        part = self.buf.at[half, pl.ds(first, count)]
+        return remote(part, part, self.send.at[n], self.recv.at[n], self.place.device(**target))
+
+    def start(self, stage):
+        for half in range(2):
+            for step in (1, 2, 3):
+                self.move(half, stage, step, 0).start()
         if stage == 2:
-            return (core * 4 + (x - back + 4) % 4) * 16, 16
-        return (core + back) % 2 * 64, 64
-
-    def copy(self, stage, step, back):
-        first, count = self.span(stage, back)
-        part = self.buf.at[pl.ds(first, count)]
-        target = (dict(dz=step), dict(dy=step), dict(dx=step), dict(flip=step))[stage]
-        n = stage * 3 + step - 1
-        return remote(part, part, self.send.at[n], self.recv.at[n], self.place.device(**target))
-
-    def steps(self, stage):
-        return (1,) if stage == 3 else (1, 2, 3)
-
-    def start(self, stage):
-        for step in self.steps(stage):
-            self.copy(stage, step, 0).start()
+            for half in range(2):
+                self.move(half, 3, 0, 0).start()
 
     def wait(self, stage):
-        for step in self.steps(stage):
-            self.copy(stage, step, step).wait_recv()
+        for half in range(2):
+            for step in (1, 2, 3):
+                self.move(half, stage, step, step).wait_recv()
+
+    def turn(self):
+        for step in (1, 3, 2):
+            for half in range(2):
+                self.move(half, 2, step, step).wait_recv()
+                self.move(half, 3, step, 0).start()
+
+    def wait_other(self):
+        for half in range(2):
+            for step in range(4):
+                self.move(half, 3, step, 0, 1).wait_recv()
 
     def finish(self):
-        for stage in range(4):
-            for step in self.steps(stage):
-                self.copy(stage, step, 0).wait_send()
+        for half in range(2):
+            for stage in range(3):
+                for step in (1, 2, 3):
+                    self.move(half, stage, step, 0).wait_send()
+            for step in range(4):
+                self.move(half, 3, step, 0).wait_send()
 
 
 class AllReduce:
@@ -248,7 +270,7 @@
 
 def step_kernel(
     res_ref, panels_ref, near_ref, len_ref, far_ref, basis_ref, coupling_ref,
-    left_ref, sums_ref, small_ref, stored_ref,
+    left_ref, sums_ref, small_ref, mixes_ref, stored_ref,
     field, space, vectors, vectors2, coeffs, coeffs2, blocks, acc, counts, rows, own, coupled, stacked,
     part, other, rings, full, part2, other2, rings2, full2, left,
     near_send, near_recv, far_send, far_recv, sum_send, sum_recv, keep_sem, load_sem, left_sem,
@@ -295,7 +317,9 @@
         first = jnp.concatenate([source[:, :B], zero], axis=0)
         second = jnp.concatenate([zero, source[:, B:]], axis=0)
         value = close(basis_ref[0], first, NT_DIMS) + close(basis_ref[1], second, NT_DIMS)
-        target[((here.core * 4 + here.x) * 4 + here.y) * 4 + here.z] = value.astype(BF16)
+        value = value.astype(BF16)
+        target.buf[0, target.slot(0)] = value[: K // 2]
+        target.buf[1, target.slot(1)] = value[K // 2 :]
 
     near_space = GroupGather(here, space, near_send.at[0], near_recv.at[0])
     near_first = GroupGather(here, vectors, near_send.at[1], near_recv.at[1])
@@ -308,11 +332,11 @@
     field[0:R, :] = res_ref[...]
     spread(res_ref, vectors, 0)
     spread(res_ref, vectors, 1)
+    project(field[0:R, :], far_first)
     pl.semaphore_wait(barrier, len(partners))
     near_space.start(2, 4, 3, 5, 0, 1)
+    far_first.start(0)
     near_first.start(2, 4, 3, 5, 0, 1)
-    project(field[0:R, :], coeffs)
-    far_first.start(0)
 
     for i in range(2):
         ids = near_ref[i : i + 1, :]
@@ -341,52 +365,45 @@
         dz = since(2) + 2 * (since(3) - since(4)) + 2 * (since(5) - since(6)) + since(6)
         return here.wide(dz, flip)
 
-    def slot_of(c):
-        late = (c + CHUNKS - KEPT) // CHUNKS
-        return c + late * (KEPT + c % 2 - c)
-
-    def keep(c):
-        return pltpu.make_async_copy(blocks.at[slot_of(c)], stored_ref.at[c - KEPT], keep_sem.at[c % 2])
-
-    def load(c):
-        return pltpu.make_async_copy(stored_ref.at[c - KEPT], blocks.at[slot_of(c)], load_sem.at[c % 2])
+    def keep(t):
+        return pltpu.make_async_copy(blocks.at[PAIRS + t % 2], stored_ref.at[t], keep_sem.at[t % 2])
+
+    def load(t):
+        return pltpu.make_async_copy(stored_ref.at[t], blocks.at[PAIRS + t % 2], load_sem.at[t % 2])
 
     def run(first, last, generate, values, events):
-        def chunk(c, carry):
+        def pair(t, carry):
             for at, event in events.items():
-                pl.when(c == at)(event)
-            w, slot, i = source_of(c), slot_of(c), row_of(c)
+                pl.when(t == at)(event)
             if generate:
-                @pl.when(c >= KEPT + 2)
+                @pl.when(t >= 2)
                 def _():
-                    keep(c - 2).wait()
+                    keep(t - 2).wait()
             elif values is vectors2:
-                @pl.when(c >= KEPT)
+                load(t).wait()
+            for c, slot in ((2 * t, PAIRS + t % 2), (2 * t + 1, t)):
+                w, i = source_of(c), row_of(c)
+                result = acc[i] if values is not None else None
+                for b in range(2):
+                    if generate:
+                        near = lax.rsqrt(fast(space[w, b], own[i], TN_DIMS)).astype(BF16)
+                        blocks[slot, b] = near
+                    else:
+                        near = blocks[slot, b]
+                    if values is not None:
+                        times = counts[i, pl.ds(w * 2 + b, 1), :][:, :1]
+                        result = result + times * fast(values[w, b], near)
+                if values is not None:
+                    acc[i] = result
+            if generate:
+                keep(t).start()
+            elif values is vectors2:
+                @pl.when(t < PAIRS - 2)
                 def _():
-                    load(c).wait()
-            result = acc[i] if values is not None else None
-            for b in range(2):
-                if generate:
-                    near = lax.rsqrt(fast(space[w, b], own[i], TN_DIMS)).astype(BF16)
-                    blocks[slot, b] = near
-                else:
-                    near = blocks[slot, b]
-                if values is not None:
-                    times = counts[i, pl.ds(w * 2 + b, 1), :][:, :1]
-                    result = result + times * fast(values[w, b], near)
-            if values is not None:
-                acc[i] = result
-            if generate:
-                @pl.when(c >= KEPT)
-                def _():
-                    keep(c).start()
-            elif values is vectors2:
-                @pl.when((c >= KEPT) & (c < CHUNKS - 2))
-                def _():
-                    load(c + 2).start()
+                    load(t + 2).start()
             return carry
 
-        lax.fori_loop(first, last, chunk, 0)
+        lax.fori_loop(first, last, pair, 0)
 
     def far_part(gathered, i):
         lane = lax.broadcasted_iota(jnp.int32, (K, 2 * R), 1)
@@ -395,8 +412,10 @@
             block = far_ref[i, n]
             device, half = block >> 1, block & 1
             wide, group = device >> 4, device & 15
-            slot = ((wide & 1) * 16 + group) * 4 + (wide >> 1)
-            value = gathered[slot].astype(F32)
+            core, z, x, y = wide & 1, wide >> 1, group >> 2, group & 3
+            value = jnp.concatenate(
+                [gathered[0, ((core * 4 + x) * 4 + y) * 4 + z], gathered[1, ((core * 4 + y) * 4 + x) * 4 + z]], axis=0
+            ).astype(F32)
             stacked[pl.ds(pl.multiple_of(n * K, K), K), :] = jnp.where(lane // R == half, value, 0.0).astype(BF16)
             return carry
 
@@ -410,176 +429,178 @@
         field[first : first + R, i * B : (i + 1) * B] = acc[i] + far_part(gathered, i)
         acc[i] = jnp.zeros((R, B), F32)
 
-    def before_2():
+    def before_1():
         near_space.wait(0, 1)
         near_first.wait(0, 1)
-
-    def before_3():
         near_space.wait(2, 4)
         near_space.start(6, 7)
         far_first.wait(0)
         far_first.start(1)
 
-    run(0, 4, True, vectors, {2: before_2, 3: before_3})
+    run(0, 2, True, vectors, {1: before_1})
+    near_space.wait(3, 5)
+    near_space.start(8, 9, 10, 11)
+    run(2, 3, True, None, {})
+    near_first.wait(2, 4)
+    near_first.start(6, 7)
+    near_first.wait(3, 5)
+    near_first.start(8, 9, 10, 11)
+    far_first.wait(1)
+    far_first.start(2)
+    run(2, 3, False, vectors, {})
 
     def before_4():
-        near_space.wait(3, 5)
-        near_space.start(8, 9, 10, 11)
-
-    def before_6():
-        near_first.wait(2, 4)
-        near_first.start(6, 7)
-        far_first.wait(1)
-        far_first.start(2)
-
-    def before_7():
         near_space.wait(6, 7)
         near_space.start(12, 13)
-
-    run(4, 8, True, None, {4: before_4, 6: before_6, 7: before_7})
-    near_first.wait(3, 5)
-    near_first.start(8, 9, 10, 11)
-    run(4, 8, False, vectors, {})
-
-    def before_8():
+        near_first.wait(6, 7)
+        near_first.start(12, 13)
         near_space.wait(8, 9, 10, 11)
         near_first.wait(8, 9, 10, 11)
-        near_first.wait(6, 7)
-        near_first.start(12, 13)
-
-    def before_10():
+
+    def before_5():
         near_space.wait(12, 13)
-        far_first.wait(2)
-        far_first.start(3)
-
-    def before_11():
         near_first.wait(12, 13)
-
-    def before_12():
-        far_first.wait(3)
+        far_first.turn()
+
+    def before_6():
+        far_first.wait_other()
         finish_row(coeffs, R, 0)
         spread(field[R : 2 * R, :], vectors2, 0)
         near_second.start(2, 5, 0)
 
-    def before_14():
+    def before_7():
         near_second.wait(2)
         near_second.start(6)
-
-    def before_15():
         near_second.wait(5)
         near_second.start(8, 10)
 
-    run(8, 16, True, vectors, {8: before_8, 10: before_10, 11: before_11, 12: before_12, 14: before_14, 15: before_15})
+    run(3, 8, True, vectors, {4: before_4, 5: before_5, 6: before_6, 7: before_7})
+    keep(PAIRS - 2).wait()
+    load(0).start()
     finish_row(coeffs, R, 1)
 
     spread(field[R : 2 * R, :], vectors2, 1)
+    project(field[R : 2 * R, :], far_second)
+    far_second.start(0)
     near_second.start(4, 3, 1)
-    keep(CHUNKS - 2).wait()
-    load(KEPT).start()
-    keep(CHUNKS - 1).wait()
-    load(KEPT + 1).start()
+    keep(PAIRS - 1).wait()
+    load(1).start()
     gram = close(field[R : 2 * R, :], field[0 : 2 * R, :], NT_DIMS) * (1.0 / total)
-    first_gram = close(field[0:R, :], field[0:R, :], NT_DIMS) * (1.0 / total)
-    part[...] = pack(gram, first_gram)
+    part[...] = pack(gram, close(field[0:R, :], field[0:R, :], NT_DIMS) * (1.0 / total))
     sum_first.start()
-    project(field[R : 2 * R, :], coeffs2)
-    far_second.start(0)
-
-    def second_2():
+
+    def second_1():
+        near_second.wait(0, 1)
         sum_first.ring(0)
-        near_second.wait(0, 1)
-
-    def second_4():
         far_second.wait(0)
         far_second.start(1)
+
+    def second_2():
         near_second.wait(4)
         near_second.start(7)
         near_second.wait(3)
         near_second.start(9, 11)
         near_second.wait(6)
         near_second.start(12)
+
+    def second_3():
         sum_first.ring(1)
-
-    def second_8():
-        near_second.wait(8, 9, 10, 11)
         far_second.wait(1)
         far_second.start(2)
 
-    def second_9():
-        sum_first.ring(2)
-
-    def second_10():
+    def second_4():
         near_second.wait(7)
         near_second.start(13)
-
-    def second_11():
+        near_second.wait(8, 9, 10, 11)
+
+    def second_5():
         near_second.wait(12, 13)
-
-    def second_14():
-        sum_first.ring(3)
+        sum_first.ring(2)
+
+    def second_7():
+        far_second.turn()
 
     run(
-        0, 16, False, vectors2,
-        {2: second_2, 4: second_4, 8: second_8, 9: second_9, 10: second_10, 11: second_11, 14: second_14},
+        0, 8, False, vectors2,
+        {1: second_1, 2: second_2, 3: second_3, 4: second_4, 5: second_5, 7: second_7},
     )
-    far_second.wait(2)
-    far_second.start(3)
+    sum_first.ring(3)
+    far_second.wait_other()
+    finish_row(coeffs2, 2 * R, 0)
+    finish_row(coeffs2, 2 * R, 1)
+
+    newest = field[2 * R :, :]
+    cross = close(newest, field[0 : 2 * R, :], NT_DIMS) * (1.0 / total)
+    part2[...] = pack(cross, close(newest, newest, NT_DIMS) * (1.0 / total))
+    sum_second.start()
     sum_first.wait()
     gram, first_gram = unpack(full[...])
+    sum_second.ring(0)
     inverse0, upper0 = cholesky(first_gram)
-    cross = gram[:, :R]
     square = pltpu.roll(gram, R, 1)[:, :R]
-    cross = exact(exact(inverse0, cross), inverse0, NT_DIMS)
+    cross = exact(exact(inverse0, gram[:, :R]), inverse0, NT_DIMS)
     square = exact(exact(inverse0, square), inverse0, NT_DIMS) - exact(cross, cross, NT_DIMS)
-    inverse1, upper1 = cholesky(jnp.concatenate([square, jnp.zeros((R, R), F32)], axis=1))
-    mix_new = exact(inverse1, inverse0)
-    mix_old = exact(exact(inverse1, cross), inverse0)
     small_ref[0] = upper0
     small_ref[1] = cross
+    small_ref[3] = inverse0
+    left[0:R, :] = close(inverse0, field[0:R, :])
+    sum_second.ring(1)
+    inverse1, upper1 = cholesky(jnp.concatenate([square, jnp.zeros((R, R), F32)], axis=1))
     small_ref[2] = upper1
-    left[0:R, :] = close(inverse0, field[0:R, :])
-    mix = jnp.concatenate([-mix_old, mix_new], axis=1)
+    mix = jnp.concatenate([-exact(exact(inverse1, cross), inverse0), exact(inverse1, inverse0)], axis=1)
+    mixes_ref[0] = gram
+    mixes_ref[1] = mix
     left[R : 2 * R, :] = close(mix, field[0 : 2 * R, :])
     early = pltpu.make_async_copy(left.at[pl.ds(0, 2 * R)], left_ref.at[pl.ds(0, 2 * R)], left_sem.at[0])
     early.start()
-    far_second.wait(3)
-    finish_row(coeffs2, 2 * R, 0)
-    finish_row(coeffs2, 2 * R, 1)
-
+    sum_second.ring(2)
     left[2 * R :, :] = close(mix, field[R:, :])
-    newest = left[2 * R :, :]
     late = pltpu.make_async_copy(left.at[pl.ds(2 * R, R)], left_ref.at[pl.ds(2 * R, R)], left_sem.at[1])
     late.start()
-    heads = close(newest, left[0 : 2 * R, :], NT_DIMS) * (1.0 / total)
-    part2[...] = pack(heads, close(newest, newest, NT_DIMS) * (1.0 / total))
-    sum_second.start()
-    for stage in range(4):
-        sum_second.ring(stage)
     for gather in (near_space, near_first, near_second, far_first, far_second, sum_first):
         gather.finish()
     early.wait()
     late.wait()
+    sum_second.ring(3)
     sum_second.wait()
     sums_ref[...] = full2[...]
     sum_second.finish()
 
 
-def last_kernel(left_ref, sums_ref, small_ref, one_ref, two_ref, factors_ref):
-    one_ref[...] = left_ref[R : 2 * R, :]
-    heads, rest = unpack(sums_ref[...])
-    rest = rest[:, :R] - exact(heads, heads, NT_DIMS)
+def last_kernel(left_hbm, sums_ref, small_ref, mixes_ref, one_ref, two_ref, factors_ref, left_ref, sem):
+    fetch = pltpu.make_async_copy(left_hbm, left_ref, sem.at[0])
+    fetch.start()
+    hand_on = pltpu.make_async_copy(left_ref.at[pl.ds(R, R)], one_ref, sem.at[1])
+    inverse0 = small_ref[3]
+    gram, mix = mixes_ref[0], mixes_ref[1]
+    cross, square = unpack(sums_ref[...])
+    pair = exact(mix, jnp.concatenate([gram, cross], axis=0))
+    heads0 = exact(pair[:, :R], inverse0, NT_DIMS)
+    heads1 = exact(pair, mix, NT_DIMS)
+    cross = pltpu.roll(cross, R, 1)[:, :R]
+    square = jnp.concatenate(
+        [
+            jnp.concatenate([pltpu.roll(gram, R, 1)[:, :R], cross.T], axis=1),
+            jnp.concatenate([cross, square[:, :R]], axis=1),
+        ],
+        axis=0,
+    )
+    rest = exact(exact(mix, square), mix, NT_DIMS) - exact(heads0, heads0, NT_DIMS) - exact(heads1, heads1, NT_DIMS)
+    fetch.wait()
+    hand_on.start()
     inverse, upper = cholesky(jnp.concatenate([rest, jnp.zeros((R, R), F32)], axis=1))
-    mix = jnp.concatenate([-exact(inverse, heads[:, :R]), -exact(inverse, pltpu.roll(heads, R, 1)[:, :R])], axis=1)
-    two_ref[...] = close(mix, left_ref[: 2 * R, :]) + close(inverse, left_ref[2 * R :, :])
+    last = jnp.concatenate([-exact(inverse, heads0), -exact(inverse, heads1)], axis=1)
+    two_ref[...] = close(last, left_ref[: 2 * R, :]) + close(inverse, left_ref[2 * R :, :])
     row = lax.broadcasted_iota(jnp.int32, (R, R), 0)
     lane = lax.broadcasted_iota(jnp.int32, (R, R), 1)
     half = jnp.where(row == lane, 0.5, 0.0)
     factors_ref[0] = small_ref[0].T
     factors_ref[1] = small_ref[1].T + half
     factors_ref[2] = small_ref[2].T
-    factors_ref[3] = heads[:, :R].T
-    factors_ref[4] = pltpu.roll(heads, R, 1)[:, :R].T + half
+    factors_ref[3] = heads0.T
+    factors_ref[4] = heads1.T + half
     factors_ref[5] = upper.T
+    hand_on.wait()
 
 
 def on_device(residual, panels, near_list, near_len, far_list, basis_far, coupling):
@@ -592,24 +613,25 @@
         pltpu.VMEM((3, 4, 48, 2 * R), F32),
         pltpu.VMEM((2, 48, 2 * R), F32),
     ]
-    left, sums_all, small, _ = pl.pallas_call(
+    left, sums_all, small, mixes, _ = pl.pallas_call(
         step_kernel,
         out_shape=(
             jax.ShapeDtypeStruct((3 * R, 2 * B), F32),
             jax.ShapeDtypeStruct((2, 48, 2 * R), F32),
-            jax.ShapeDtypeStruct((3, R, R), F32),
-            jax.ShapeDtypeStruct((CHUNKS - KEPT, 2, B, B), BF16),
+            jax.ShapeDtypeStruct((4, R, R), F32),
+            jax.ShapeDtypeStruct((2, R, 2 * R), F32),
+            jax.ShapeDtypeStruct((PAIRS, 2, B, B), BF16),
         ),
         in_specs=[vmem, vmem, vmem, smem, smem, vmem, vmem],
-        out_specs=(pl.BlockSpec(memory_space=pl.ANY), vmem, vmem, pl.BlockSpec(memory_space=pl.ANY)),
+        out_specs=(pl.BlockSpec(memory_space=pl.ANY), vmem, vmem, vmem, pl.BlockSpec(memory_space=pl.ANY)),
         scratch_shapes=[
             pltpu.VMEM((3 * R, 2 * B), F32),
             pltpu.VMEM((8, 2, DEPTH, B), BF16),
             pltpu.VMEM((8, 2, R, B), BF16),
             pltpu.VMEM((8, 2, R, B), BF16),
-            pltpu.VMEM((128, K, 2 * R), BF16),
-            pltpu.VMEM((128, K, 2 * R), BF16),
-            pltpu.VMEM((KEPT + 2, 2, B, B), BF16),
+            pltpu.VMEM((2, 128, K // 2, 2 * R), BF16),
+            pltpu.VMEM((2, 128, K // 2, 2 * R), BF16),
+            pltpu.VMEM((PAIRS + 2, 2, B, B), BF16),
             pltpu.VMEM((2, R, B), F32),
             pltpu.VMEM((2, 16, 128), F32),
             pltpu.VMEM((2, DEPTH, B), F32),
@@ -621,8 +643,8 @@
             pltpu.VMEM((3 * R, 2 * B), F32),
             pltpu.SemaphoreType.DMA((3, 14)),
             pltpu.SemaphoreType.DMA((3, 14)),
-            pltpu.SemaphoreType.DMA((2, 10)),
-            pltpu.SemaphoreType.DMA((2, 10)),
+            pltpu.SemaphoreType.DMA((2, 26)),
+            pltpu.SemaphoreType.DMA((2, 26)),
             pltpu.SemaphoreType.DMA((2, 11)),
             pltpu.SemaphoreType.DMA((2, 11)),
             pltpu.SemaphoreType.DMA((2,)),
@@ -637,10 +659,11 @@
     one, two, factors = pl.pallas_call(
         last_kernel,
         out_shape=(wide, wide, jax.ShapeDtypeStruct((6, R, R), F32)),
-        in_specs=[vmem, vmem, vmem],
-        out_specs=(vmem, vmem, vmem),
+        in_specs=[pl.BlockSpec(memory_space=pl.ANY), vmem, vmem, vmem],
+        out_specs=(pl.BlockSpec(memory_space=pl.ANY), vmem, vmem),
+        scratch_shapes=[pltpu.VMEM((3 * R, 2 * B), F32), pltpu.SemaphoreType.DMA((2,))],
         cost_estimate=pl.CostEstimate(flops=150_000_000, bytes_accessed=3_000_000, transcendentals=64),
-    )(left, sums_all, small)
+    )(left, sums_all, small, mixes)
     return (one.T, two.T, factors)
 
 

time: 104 us -> 91.7 us (0.88)
  Pallas kernels: 103 us -> 90.5 us
    pallas_call x1, Pallas kernels: 98.2 us -> 84.7 us  [on_device(): pl.pallas_call(step_kernel, out_shape=(jax.ShapeDtypeStruct((3 * R, 2 * B...]
where the time goes in v4:
time: 91.7 us; the launch traced here: 91.3 us
  Pallas kernels  90.5 us (99%)
    pallas_call x1, Pallas kernels, on_device(): pl.pallas_call(step_kernel, out_shape=(jax.ShapeDtypeStruct((3 * R, 2 * B...  84.7 us
    pallas_call x1, Pallas kernels, on_device(): pl.pallas_call(last_kernel, out_shape=(wide, wide, jax.ShapeDtypeStruct((...  5.76 us

profile of v4, /device:TPU:1, one launch (start us, length us, event | category | flops | bytes accessed | tf_op | source)
XLA Modules:
  0.0 91.3 jit_solution(7748582443633730971)
XLA Ops:
  0.6 84.7 %shard_map.94 = (f32[192,2048]{1,0:T(8,128)}, f32[2,48,128]{2,1,0:T(8,128)}, f32[4,64,64]{2,1,0:T(8,128)}, f32[2,64,128]{2,1,0:T(8,128)}, bf16[8,2,1024,1024]{3,2,1,0:T(8,128)(2,1)}) custom-call(f32[64,2048]{1,0:T(8,128)} %bitcast.3, f32[2,4,1024]{2,1,0:T(4,128)} %panels_ref.1, s32[2,16]{1,0:T(2,128)} %near_ref.1, s32[2]{0:T(128)} %len_ref.1, ...), custom_call_target="tpu_custom_call" | custom-call | flops 16999999488 | bytes 80000000 | tf_op jit(solution)/shard_map/pallas_call | solution.py:616
  85.4 5.8 %shard_map.95 = (f32[64,2048]{1,0:T(8,128)}, f32[64,2048]{1,0:T(8,128)}, f32[6,64,64]{2,1,0:T(8,128)}) custom-call(f32[192,2048]{1,0:T(8,128)} %get-tuple-element.10.left_hbm, f32[2,48,128]{2,1,0:T(8,128)} %get-tuple-element.11.sums_ref, f32[4,64,64]{2,1,0:T(8,128)} %get-tuple-element.12.small_ref, f32[2,64,128]{2,1,0:T(8,128)} %get-tuple-element.13.mixes_ref), custom_call_target="tpu_custom_call" | custom-call | flops 150000000 | bytes 3000000 | tf_op jit(solution)/shard_map/pallas_call | solution.py:659

commit v5 on v4

--- a/solution.py
+++ b/solution.py
@@ -175,58 +175,77 @@
 
 
 class AllReduce:
-    def __init__(self, place, part, other, rings, full, send, recv):
-        self.place, self.part, self.other, self.rings, self.full = place, part, other, rings, full
+    PEERS = tuple((dz, flip) for dz in range(4) for flip in range(2) if dz + flip)
+
+    def __init__(self, place, part, pieces, rings, full, send, recv):
+        self.place, self.part, self.pieces, self.rings, self.full = place, part, pieces, rings, full
         self.send, self.recv = send, recv
 
-    def swap(self):
+    def scatter(self, n):
         here = self.place
+        dz, flip = self.PEERS[n]
         return remote(
-            self.part.at[1 - here.core], self.other, self.send.at[0], self.recv.at[0], here.device(flip=1)
+            self.part.at[here.wide(dz, flip)], self.pieces.at[here.wide(0, 0)],
+            self.send.at[n], self.recv.at[n], here.device(dz, flip),
         )
 
-    def spot(self, stage):
-        return (self.place.z, self.place.y, self.place.x)[stage]
-
     def copy(self, stage, step, back):
-        slot = self.rings.at[stage, (self.spot(stage) - back + 4) % 4]
-        target = (dict(dz=step), dict(dy=step), dict(dx=step))[stage]
-        n = 1 + stage * 3 + step - 1
-        return remote(slot, slot, self.send.at[n], self.recv.at[n], self.place.device(**target))
-
-    def share(self, back):
-        half = self.full.at[(self.place.core + back) % 2]
-        return remote(half, half, self.send.at[10], self.recv.at[10], self.place.device(flip=1))
+        here = self.place
+        slot = self.rings.at[stage, ((here.y, here.x)[stage] - back + 4) % 4]
+        target = (dict(dy=step), dict(dx=step))[stage]
+        n = 7 + stage * 3 + step - 1
+        return remote(slot, slot, self.send.at[n], self.recv.at[n], here.device(**target))
+
+    def share(self, n):
+        here = self.place
+        dz, flip = self.PEERS[n]
+        piece = self.full.at[here.wide(0, 0)]
+        return remote(piece, piece, self.send.at[13 + n], self.recv.at[13 + n], here.device(dz, flip))
+
+    def arrival(self, buffer, n, sem):
+        here = self.place
+        dz, flip = self.PEERS[n]
+        piece = buffer.at[here.wide(-dz, flip)]
+        return remote(piece, piece, self.send.at[sem], self.recv.at[sem], here.device(dz, flip))
 
     def start(self):
-        self.swap().start()
+        for n in range(7):
+            self.scatter(n).start()
 
     def ring(self, stage):
+        here = self.place
         if stage == 0:
-            self.swap().wait_recv()
-            total = self.part[self.place.core] + self.other[...]
+            for n in range(7):
+                self.arrival(self.pieces, n, n).wait_recv()
+            p = self.pieces
+            me = here.wide(0, 0)
+            p[me] = self.part[me]
+            total = ((p[0] + p[1]) + (p[2] + p[3])) + ((p[4] + p[5]) + (p[6] + p[7]))
         else:
             for step in (1, 2, 3):
                 self.copy(stage - 1, step, step).wait_recv()
             rings = self.rings
             total = (rings[stage - 1, 0] + rings[stage - 1, 1]) + (rings[stage - 1, 2] + rings[stage - 1, 3])
-        if stage < 3:
-            self.rings[stage, self.spot(stage)] = total
+        if stage < 2:
+            self.rings[stage, (here.y, here.x)[stage]] = total
             for step in (1, 2, 3):
                 self.copy(stage, step, 0).start()
         else:
-            self.full[self.place.core] = total
-            self.share(0).start()
+            self.full[here.wide(0, 0)] = total
+            for n in range(7):
+                self.share(n).start()
 
     def wait(self):
-        self.share(1).wait_recv()
+        for n in range(7):
+            self.arrival(self.full, n, 13 + n).wait_recv()
 
     def finish(self):
-        self.swap().wait_send()
-        for stage in range(3):
+        for n in range(7):
+            self.scatter(n).wait_send()
+            self.share(n).wait_send()
+        for stage in range(2):
             for step in (1, 2, 3):
                 self.copy(stage, step, 0).wait_send()
-        self.share(0).wait_send()
 
 
 def cholesky(gram):
@@ -258,22 +277,21 @@
 
 
 def pack(wide, square):
-    low = jnp.concatenate([square[: R // 2], square[R // 2 :]], axis=1)
-    return jnp.concatenate([wide, low], axis=0).reshape(2, 48, 2 * R)
+    return jnp.concatenate([wide, jnp.concatenate([square, square], axis=1)], axis=0).reshape(8, 16, 2 * R)
 
 
 def unpack(value):
-    value = value.reshape(96, 2 * R)
-    low = value[R:]
-    return value[:R], jnp.concatenate([low, pltpu.roll(low, R, 1)], axis=0)
+    value = value.reshape(2 * R, 2 * R)
+    return value[:R], value[R:]
 
 
 def step_kernel(
-    res_ref, panels_ref, near_ref, len_ref, far_ref, basis_ref, coupling_ref,
+    res_hbm, panels_hbm, near_ref, len_ref, far_ref, far_vec_ref, basis_hbm, coupling_hbm,
     left_ref, sums_ref, small_ref, mixes_ref, stored_ref,
     field, space, vectors, vectors2, coeffs, coeffs2, blocks, acc, counts, rows, own, coupled, stacked,
     part, other, rings, full, part2, other2, rings2, full2, left,
     near_send, near_recv, far_send, far_recv, sum_send, sum_recv, keep_sem, load_sem, left_sem,
+    res_ref, panels_ref, basis_ref, coupling_ref, input_sem,
 ):
     here = Place()
     me = here.wide(0, 0)
@@ -282,9 +300,19 @@
     barrier = pltpu.get_barrier_semaphore()
     partners = [here.device(flip=1)]
     for step in (1, 2, 3):
-        partners += [here.device(dz=step), here.device(dy=step), here.device(dx=step)]
+        partners += [here.device(dz=step), here.device(dz=step, flip=1), here.device(dy=step), here.device(dx=step)]
     for partner in partners:
         pl.semaphore_signal(barrier, inc=1, device_id=partner, device_id_type=MESH)
+
+    inputs = [
+        pltpu.make_async_copy(source, target, input_sem.at[n])
+        for n, (source, target) in enumerate(
+            ((panels_hbm, panels_ref), (res_hbm, res_ref), (basis_hbm, basis_ref), (coupling_hbm, coupling_ref))
+        )
+    ]
+    for copy in inputs:
+        copy.start()
+    inputs[0].wait()
 
     for b in range(2):
         point = [panels_ref[b, a : a + 1, :] for a in range(3)]
@@ -329,15 +357,13 @@
     sum_first = AllReduce(here, part, other, rings, full, sum_send.at[0], sum_recv.at[0])
     sum_second = AllReduce(here, part2, other2, rings2, full2, sum_send.at[1], sum_recv.at[1])
 
+    inputs[1].wait()
     field[0:R, :] = res_ref[...]
     spread(res_ref, vectors, 0)
     spread(res_ref, vectors, 1)
+    inputs[2].wait()
     project(field[0:R, :], far_first)
-    pl.semaphore_wait(barrier, len(partners))
-    near_space.start(2, 4, 3, 5, 0, 1)
-    far_first.start(0)
-    near_first.start(2, 4, 3, 5, 0, 1)
-
+    inputs[3].wait()
     for i in range(2):
         ids = near_ref[i : i + 1, :]
         ids = (ids >> 5) * 2 + (ids & 1)
@@ -345,10 +371,20 @@
         slot = lax.broadcasted_iota(jnp.int32, (16, 16), 1)
         hit = jnp.where((ids == wanted) & (slot < len_ref[i]), 1.0, 0.0)
         counts[i] = jnp.broadcast_to(jnp.sum(hit, axis=1, keepdims=True), (16, 128))
-        high, low = two_parts(coupling_ref[i])
-        coupled[i, :K] = high
-        coupled[i, K:] = low
+        odd = jnp.broadcast_to(far_vec_ref[i : i + 1, :] & 1, (8, NF)).astype(F32)
+        spot = lax.broadcasted_iota(jnp.int32, (NF, NF * K), 1) // K
+        entry = lax.broadcasted_iota(jnp.int32, (NF, NF * K), 0)
+        odd = fast(odd.astype(BF16), jnp.where(spot == entry, 1.0, 0.0).astype(BF16))[0:1]
+        for at, keep_it in ((0, 1.0 - odd), (2 * K, odd)):
+            high, low = two_parts(coupling_ref[i] * keep_it)
+            coupled[i, at : at + K] = high
+            coupled[i, at + K : at + 2 * K] = low
         acc[i] = jnp.zeros((R, B), F32)
+
+    pl.semaphore_wait(barrier, len(partners))
+    near_space.start(2, 4, 3, 5, 0, 1)
+    far_first.start(0)
+    near_first.start(2, 4, 3, 5, 0, 1)
 
     def row_of(c):
         late = c // 8
@@ -406,22 +442,20 @@
         lax.fori_loop(first, last, pair, 0)
 
     def far_part(gathered, i):
-        lane = lax.broadcasted_iota(jnp.int32, (K, 2 * R), 1)
-
         def entry(n, carry):
-            block = far_ref[i, n]
-            device, half = block >> 1, block & 1
+            device = far_ref[i, n] >> 1
             wide, group = device >> 4, device & 15
             core, z, x, y = wide & 1, wide >> 1, group >> 2, group & 3
-            value = jnp.concatenate(
-                [gathered[0, ((core * 4 + x) * 4 + y) * 4 + z], gathered[1, ((core * 4 + y) * 4 + x) * 4 + z]], axis=0
-            ).astype(F32)
-            stacked[pl.ds(pl.multiple_of(n * K, K), K), :] = jnp.where(lane // R == half, value, 0.0).astype(BF16)
+            stacked[pl.ds(pl.multiple_of(n * K, K), K // 2), :] = gathered[0, ((core * 4 + x) * 4 + y) * 4 + z]
+            stacked[pl.ds(pl.multiple_of(n * K + K // 2, K // 2), K // 2), :] = gathered[
+                1, ((core * 4 + y) * 4 + x) * 4 + z
+            ]
             return carry
 
         lax.fori_loop(0, NF, entry, 0, unroll=8)
         inside = fast(coupled[i], stacked[...])
-        inside = inside[:K] + inside[K:]
+        first = lax.broadcasted_iota(jnp.int32, (K, 2 * R), 1) < R
+        inside = jnp.where(first, inside[:K] + inside[K : 2 * K], inside[2 * K : 3 * K] + inside[3 * K :])
         result = close(inside, basis_ref[i], TN_DIMS)
         return result[:R] + result[R:]
 
@@ -434,20 +468,20 @@
         near_first.wait(0, 1)
         near_space.wait(2, 4)
         near_space.start(6, 7)
-        far_first.wait(0)
-        far_first.start(1)
 
     run(0, 2, True, vectors, {1: before_1})
     near_space.wait(3, 5)
     near_space.start(8, 9, 10, 11)
+    far_first.wait(0)
+    far_first.start(1)
     run(2, 3, True, None, {})
     near_first.wait(2, 4)
     near_first.start(6, 7)
     near_first.wait(3, 5)
     near_first.start(8, 9, 10, 11)
+    run(2, 3, False, vectors, {})
     far_first.wait(1)
     far_first.start(2)
-    run(2, 3, False, vectors, {})
 
     def before_4():
         near_space.wait(6, 7)
@@ -491,7 +525,6 @@
 
     def second_1():
         near_second.wait(0, 1)
-        sum_first.ring(0)
         far_second.wait(0)
         far_second.start(1)
 
@@ -504,7 +537,7 @@
         near_second.start(12)
 
     def second_3():
-        sum_first.ring(1)
+        sum_first.ring(0)
         far_second.wait(1)
         far_second.start(2)
 
@@ -515,16 +548,16 @@
 
     def second_5():
         near_second.wait(12, 13)
-        sum_first.ring(2)
+        sum_first.ring(1)
 
     def second_7():
         far_second.turn()
+        sum_first.ring(2)
 
     run(
         0, 8, False, vectors2,
         {1: second_1, 2: second_2, 3: second_3, 4: second_4, 5: second_5, 7: second_7},
     )
-    sum_first.ring(3)
     far_second.wait_other()
     finish_row(coeffs2, 2 * R, 0)
     finish_row(coeffs2, 2 * R, 1)
@@ -535,14 +568,14 @@
     sum_second.start()
     sum_first.wait()
     gram, first_gram = unpack(full[...])
+    inverse0, upper0 = cholesky(first_gram)
+    small_ref[0] = upper0
+    small_ref[3] = inverse0
     sum_second.ring(0)
-    inverse0, upper0 = cholesky(first_gram)
-    square = pltpu.roll(gram, R, 1)[:, :R]
-    cross = exact(exact(inverse0, gram[:, :R]), inverse0, NT_DIMS)
-    square = exact(exact(inverse0, square), inverse0, NT_DIMS) - exact(cross, cross, NT_DIMS)
-    small_ref[0] = upper0
+    both = exact(inverse0, gram)
+    cross = exact(both[:, :R], inverse0, NT_DIMS)
+    square = exact(pltpu.roll(both, R, 1)[:, :R], inverse0, NT_DIMS) - exact(cross, cross, NT_DIMS)
     small_ref[1] = cross
-    small_ref[3] = inverse0
     left[0:R, :] = close(inverse0, field[0:R, :])
     sum_second.ring(1)
     inverse1, upper1 = cholesky(jnp.concatenate([square, jnp.zeros((R, R), F32)], axis=1))
@@ -550,10 +583,10 @@
     mix = jnp.concatenate([-exact(exact(inverse1, cross), inverse0), exact(inverse1, inverse0)], axis=1)
     mixes_ref[0] = gram
     mixes_ref[1] = mix
+    sum_second.ring(2)
     left[R : 2 * R, :] = close(mix, field[0 : 2 * R, :])
     early = pltpu.make_async_copy(left.at[pl.ds(0, 2 * R)], left_ref.at[pl.ds(0, 2 * R)], left_sem.at[0])
     early.start()
-    sum_second.ring(2)
     left[2 * R :, :] = close(mix, field[R:, :])
     late = pltpu.make_async_copy(left.at[pl.ds(2 * R, R)], left_ref.at[pl.ds(2 * R, R)], left_sem.at[1])
     late.start()
@@ -561,7 +594,6 @@
         gather.finish()
     early.wait()
     late.wait()
-    sum_second.ring(3)
     sum_second.wait()
     sums_ref[...] = full2[...]
     sum_second.finish()
@@ -589,7 +621,7 @@
     fetch.wait()
     hand_on.start()
     inverse, upper = cholesky(jnp.concatenate([rest, jnp.zeros((R, R), F32)], axis=1))
-    last = jnp.concatenate([-exact(inverse, heads0), -exact(inverse, heads1)], axis=1)
+    last = jnp.concatenate([-close(inverse, heads0), -close(inverse, heads1)], axis=1)
     two_ref[...] = close(last, left_ref[: 2 * R, :]) + close(inverse, left_ref[2 * R :, :])
     row = lax.broadcasted_iota(jnp.int32, (R, R), 0)
     lane = lax.broadcasted_iota(jnp.int32, (R, R), 1)
@@ -606,23 +638,24 @@
 def on_device(residual, panels, near_list, near_len, far_list, basis_far, coupling):
     vmem = pl.BlockSpec(memory_space=pltpu.VMEM)
     smem = pl.BlockSpec(memory_space=pltpu.SMEM)
+    hbm = pl.BlockSpec(memory_space=pl.ANY)
     wide = jax.ShapeDtypeStruct((R, 2 * B), F32)
     sums = [
-        pltpu.VMEM((2, 48, 2 * R), F32),
-        pltpu.VMEM((48, 2 * R), F32),
-        pltpu.VMEM((3, 4, 48, 2 * R), F32),
-        pltpu.VMEM((2, 48, 2 * R), F32),
+        pltpu.VMEM((8, 16, 2 * R), F32),
+        pltpu.VMEM((8, 16, 2 * R), F32),
+        pltpu.VMEM((2, 4, 16, 2 * R), F32),
+        pltpu.VMEM((8, 16, 2 * R), F32),
     ]
     left, sums_all, small, mixes, _ = pl.pallas_call(
         step_kernel,
         out_shape=(
             jax.ShapeDtypeStruct((3 * R, 2 * B), F32),
-            jax.ShapeDtypeStruct((2, 48, 2 * R), F32),
+            jax.ShapeDtypeStruct((8, 16, 2 * R), F32),
             jax.ShapeDtypeStruct((4, R, R), F32),
             jax.ShapeDtypeStruct((2, R, 2 * R), F32),
             jax.ShapeDtypeStruct((PAIRS, 2, B, B), BF16),
         ),
-        in_specs=[vmem, vmem, vmem, smem, smem, vmem, vmem],
+        in_specs=[hbm, hbm, vmem, smem, smem, vmem, hbm, hbm],
         out_specs=(pl.BlockSpec(memory_space=pl.ANY), vmem, vmem, vmem, pl.BlockSpec(memory_space=pl.ANY)),
         scratch_shapes=[
             pltpu.VMEM((3 * R, 2 * B), F32),
@@ -636,7 +669,7 @@
             pltpu.VMEM((2, 16, 128), F32),
             pltpu.VMEM((2, DEPTH, B), F32),
             pltpu.VMEM((2, DEPTH, B), BF16),
-            pltpu.VMEM((2, 2 * K, NF * K), BF16),
+            pltpu.VMEM((2, 4 * K, NF * K), BF16),
             pltpu.VMEM((NF * K, 2 * R), BF16),
             *sums,
             *sums,
@@ -645,17 +678,22 @@
             pltpu.SemaphoreType.DMA((3, 14)),
             pltpu.SemaphoreType.DMA((2, 26)),
             pltpu.SemaphoreType.DMA((2, 26)),
-            pltpu.SemaphoreType.DMA((2, 11)),
-            pltpu.SemaphoreType.DMA((2, 11)),
+            pltpu.SemaphoreType.DMA((2, 20)),
+            pltpu.SemaphoreType.DMA((2, 20)),
             pltpu.SemaphoreType.DMA((2,)),
             pltpu.SemaphoreType.DMA((2,)),
             pltpu.SemaphoreType.DMA((2,)),
+            pltpu.VMEM((R, 2 * B), F32),
+            pltpu.VMEM((2, 4, B), F32),
+            pltpu.VMEM((2, K, B), F32),
+            pltpu.VMEM((2, K, NF * K), F32),
+            pltpu.SemaphoreType.DMA((4,)),
         ],
         compiler_params=pltpu.CompilerParams(
             collective_id=0, has_side_effects=True, vmem_limit_bytes=62 * 2**20
         ),
         cost_estimate=pl.CostEstimate(flops=17_000_000_000, bytes_accessed=80_000_000, transcendentals=33_554_432),
-    )(residual.T, panels, near_list, near_len, far_list, basis_far, coupling)
+    )(residual.T, panels, near_list, near_len, far_list, far_list, basis_far, coupling)
     one, two, factors = pl.pallas_call(
         last_kernel,
         out_shape=(wide, wide, jax.ShapeDtypeStruct((6, R, R), F32)),

time: 91.7 us -> 91 us (level)
  no operation moved by 1% of the time
where the time goes in v5:
time: 91 us; the launch traced here: 90.6 us
  Pallas kernels  89.8 us (99%)
    pallas_call x1, Pallas kernels, on_device(): pl.pallas_call(step_kernel, out_shape=(jax.ShapeDtypeStruct((3 * R, 2 * B...  84 us
    pallas_call x1, Pallas kernels, on_device(): pl.pallas_call(last_kernel, out_shape=(wide, wide, jax.ShapeDtypeStruct((...  5.8 us

profile of v5, /device:TPU:1, one launch (start us, length us, event | category | flops | bytes accessed | tf_op | source)
XLA Modules:
  0.0 90.6 jit_solution(2914352962335354688)
XLA Ops:
  0.6 84.0 %shard_map.94 = (f32[192,2048]{1,0:T(8,128)}, f32[8,16,128]{2,1,0:T(8,128)}, f32[4,64,64]{2,1,0:T(8,128)}, f32[2,64,128]{2,1,0:T(8,128)}, bf16[8,2,1024,1024]{3,2,1,0:T(8,128)(2,1)}) custom-call(f32[64,2048]{1,0:T(8,128)} %bitcast.3, f32[2,4,1024]{2,1,0:T(4,128)} %panels_hbm.1, s32[2,16]{1,0:T(2,128)} %near_ref.1, s32[2]{0:T(128)} %len_ref.1, ...), custom_call_target="tpu_custom_call" | custom-call | flops 16999999488 | bytes 80000000 | tf_op jit(solution)/shard_map/pallas_call | solution.py:649
  84.7 5.8 %shard_map.95 = (f32[64,2048]{1,0:T(8,128)}, f32[64,2048]{1,0:T(8,128)}, f32[6,64,64]{2,1,0:T(8,128)}) custom-call(f32[192,2048]{1,0:T(8,128)} %get-tuple-element.10.left_hbm, f32[8,16,128]{2,1,0:T(8,128)} %get-tuple-element.11.sums_ref, f32[4,64,64]{2,1,0:T(8,128)} %get-tuple-element.12.small_ref, f32[2,64,128]{2,1,0:T(8,128)} %get-tuple-element.13.mixes_ref), custom_call_target="tpu_custom_call" | custom-call | flops 150000000 | bytes 3000000 | tf_op jit(solution)/shard_map/pallas_call | solution.py:697
